TPU v7x, 128 devices: a whole 4x4x4 slice. The times are simulated.
128 devices in a mesh: dp: 8 (over x, core), seq: 16 (over y, z).
Axes of the slice: x: 4, y: 4, z: 4, core: 2. Of those that a mesh axis runs over, the one named last changes fastest.
Arguments:
- queries: bfloat16 [8, 2048, 1024], P('dp', 'seq'), may hold values from -6 to 6
- key_vectors: bfloat16 [8, 2048, 2, 1024], P('dp', 'seq'), may hold values from -6 to 6
- values: bfloat16 [8, 2048, 2, 1024], P('dp', 'seq'), may hold values from -0.08984375 to 0.08984375
- beta_raw: float32 [8, 2048, 16], P('dp', 'seq'), may hold values from -2 to 12
- cotangent: bfloat16 [8, 2048, 2048], P('dp', 'seq'), may hold values from -6 to 6
- w_out: bfloat16 [1024, 2048], P(('dp', 'seq')), may hold values from -0.1875 to 0.1875
Outputs:
- projected: bfloat16 [8, 2048, 2048], P('dp', 'seq')
- grad_queries: bfloat16 [8, 2048, 1024], P('dp', 'seq')
- grad_keys: bfloat16 [8, 2048, 2, 1024], P('dp', 'seq')
- grad_values: bfloat16 [8, 2048, 2, 1024], P('dp', 'seq')
- grad_beta: float32 [8, 2048, 16], P('dp', 'seq')
- grad_w_out: float32 [1024, 2048], P(('dp', 'seq'))
All inputs are finite; a program needn't handle non-finite values.
Results may differ from a plain program's by a relative error of at most 0.013.
Values may be sent and summed in bfloat16 or wider, within the bound.
A program may use at most 192 MiB of HBM per device.

v0:
```python
import jax
import jax.numpy as jnp
from jax import lax
from jax.sharding import PartitionSpec as P

LOOKUP_DIM = 128
DV = 128
BLOCK = 64


HIGHEST_PREC = lax.Precision.HIGHEST
norm_eps = 1e-06


def passed_along(value, axis, steps):
    count = lax.axis_size(axis)
    first, last = (max(0, -steps), min(count, count - steps))
    return lax.ppermute(value, axis, [(source, source + steps) for source in range(first, last)])


def block_update(carried, pieces):
    queries, key_vectors, values, betas = pieces
    step_count = key_vectors.shape[0]
    frame_count = queries.shape[0]
    key_width = key_vectors.shape[2]
    key_inner = jnp.einsum("ihd,jhd->hij", key_vectors, key_vectors, precision=HIGHEST_PREC)
    row_index = lax.broadcasted_iota(jnp.int32, (step_count, step_count), 0)
    col_index = lax.broadcasted_iota(jnp.int32, (step_count, step_count), 1)
    below_diag = (col_index < row_index).astype(jnp.float32)
    beta_heads = jnp.transpose(betas)
    system = (
        jnp.eye(step_count, dtype=jnp.float32) + below_diag * beta_heads[:, :, None] * key_inner
    )
    stacked = jnp.concatenate(
        [jnp.transpose(key_vectors, (1, 0, 2)), jnp.transpose(values, (1, 0, 2))], axis=2
    )
    solved = jax.scipy.linalg.solve_triangular(
        system, beta_heads[:, :, None] * stacked, lower=True, unit_diagonal=True
    )
    deltas = solved[:, :, key_width:] - jnp.einsum(
        "hid,hde->hie", solved[:, :, :key_width], carried, precision=HIGHEST_PREC
    )
    scores = jnp.einsum("fhd,jhd->hfj", queries, key_vectors, precision=HIGHEST_PREC)
    frame_index = lax.broadcasted_iota(jnp.int32, (frame_count, step_count), 0)
    step_index = lax.broadcasted_iota(jnp.int32, (frame_count, step_count), 1)
    visible = (step_index // 2 <= frame_index).astype(jnp.float32)
    outputs = jnp.einsum("fhd,hde->fhe", queries, carried, precision=HIGHEST_PREC)
    outputs = outputs + jnp.einsum(
        "hfj,hje->fhe", scores * visible[None], deltas, precision=HIGHEST_PREC
    )
    carried = carried + jnp.einsum("jhd,hje->hde", key_vectors, deltas, precision=HIGHEST_PREC)
    return (carried, outputs)


def run_blocks(queries, key_vectors, values, betas, carried):
    frame_count, head_count, key_width = queries.shape
    block_count = frame_count // BLOCK
    grouped = (
        queries.reshape(block_count, BLOCK, head_count, key_width),
        key_vectors.reshape(block_count, 2 * BLOCK, head_count, key_width),
        values.reshape(block_count, 2 * BLOCK, head_count, values.shape[2]),
        betas.reshape(block_count, 2 * BLOCK, head_count),
    )
    carried, outputs = lax.scan(block_update, carried, grouped)
    return (outputs.reshape(frame_count, head_count, values.shape[2]), carried)


def prepare(queries, key_vectors, values, beta_raw):
    frame_count = queries.shape[0]
    head_count = queries.shape[1] // LOOKUP_DIM
    query_heads = queries.astype(jnp.float32).reshape(frame_count, head_count, LOOKUP_DIM)
    key_heads = key_vectors.astype(jnp.float32).reshape(2 * frame_count, head_count, LOOKUP_DIM)
    key_heads = key_heads * lax.rsqrt(
        jnp.sum(key_heads * key_heads, axis=2, keepdims=True) + norm_eps
    )
    value_heads = values.astype(jnp.float32).reshape(2 * frame_count, head_count, DV)
    betas = 2.0 * jax.nn.sigmoid(beta_raw.reshape(2 * frame_count, head_count))
    return (query_heads, key_heads, value_heads, betas)


def per_device(queries, key_vectors, values, beta_raw, cotangent, w_out):
    head_count = queries.shape[2] // LOOKUP_DIM
    frame_count = queries.shape[1]
    identity = jnp.broadcast_to(
        jnp.eye(LOOKUP_DIM, dtype=jnp.float32), (head_count, LOOKUP_DIM, LOOKUP_DIM)
    )
    empty_state = jnp.zeros((head_count, LOOKUP_DIM, DV), jnp.float32)
    cot_one = cotangent[0]

    def local_part(query_one, key_one, value_one, raw_one):
        query_heads, key_heads, value_heads, betas = prepare(query_one, key_one, value_one, raw_one)
        widened = jnp.concatenate([jnp.zeros(key_heads.shape, jnp.float32), value_heads], axis=2)
        start_state = jnp.concatenate([identity, empty_state], axis=2)
        return run_blocks(query_heads, key_heads, widened, betas, start_state)

    (outputs, final_state), pullback = jax.vjp(
        local_part, queries[0], key_vectors[0], values[0], beta_raw[0]
    )
    transit = final_state[:, :, :LOOKUP_DIM]
    offset = final_state[:, :, LOOKUP_DIM:]

    def pass_state(counter, carried):
        leaving = jnp.einsum("hdk,hke->hde", transit, carried, precision=HIGHEST_PREC) + offset
        return passed_along(leaving, "seq", 1)

    entering = lax.fori_loop(0, lax.axis_size("seq") - 1, pass_state, empty_state)
    reads = outputs[:, :, :LOOKUP_DIM]
    mixed = (
        jnp.einsum("fhd,hde->fhe", reads, entering, precision=HIGHEST_PREC)
        + outputs[:, :, LOOKUP_DIM:]
    )
    mixed = mixed.reshape(frame_count, head_count * DV)
    mixed_bf = mixed.astype(jnp.bfloat16)
    gathered = lax.all_gather(w_out, ("dp", "seq"), axis=0, tiled=True)
    projected = jnp.dot(mixed_bf, gathered, preferred_element_type=jnp.float32)
    mixed_grad = lax.dot_general(
        cot_one, gathered, (((1,), (1,)), ((), ())), preferred_element_type=jnp.float32
    )
    projected = projected.astype(jnp.bfloat16)
    grad_heads = mixed_grad.reshape(frame_count, head_count, DV)
    local_adjoint = jnp.einsum("fhd,fhe->hde", reads, grad_heads, precision=HIGHEST_PREC)
    flipped = jnp.swapaxes(transit, 1, 2)

    def pass_adjoint(counter, carried):
        sending = (
            jnp.einsum("hdk,hke->hde", flipped, carried, precision=HIGHEST_PREC) + local_adjoint
        )
        return passed_along(sending, "seq", -1)

    later_grad = lax.fori_loop(0, lax.axis_size("seq") - 1, pass_adjoint, empty_state)
    read_grad = jnp.einsum("fhe,hde->fhd", grad_heads, entering, precision=HIGHEST_PREC)
    output_grad = jnp.concatenate([read_grad, grad_heads], axis=2)
    transit_grad = jnp.einsum("hde,hke->hdk", later_grad, entering, precision=HIGHEST_PREC)
    state_grad = jnp.concatenate([transit_grad, later_grad], axis=2)
    grad_query, grad_key, grad_value, grad_raw = pullback((output_grad, state_grad))
    grad_weight = lax.psum_scatter(
        lax.dot_general(
            mixed_bf, cot_one, (((0,), (0,)), ((), ())), preferred_element_type=jnp.float32
        ),
        ("dp", "seq"),
        scatter_dimension=0,
        tiled=True,
    )
    return (
        projected[None],
        grad_query[None],
        grad_key[None],
        grad_value[None],
        grad_raw[None],
        grad_weight,
    )


def solution(mesh):
    in_specs = (
        P("dp", "seq", None),
        P("dp", "seq", None, None),
        P("dp", "seq", None, None),
        P("dp", "seq", None),
        P("dp", "seq", None),
        P(("dp", "seq"), None),
    )
    out_specs = (
        P("dp", "seq", None),
        P("dp", "seq", None),
        P("dp", "seq", None, None),
        P("dp", "seq", None, None),
        P("dp", "seq", None),
        P(("dp", "seq"), None),
    )
    return jax.shard_map(
        per_device, mesh=mesh, in_specs=in_specs, out_specs=out_specs, check_vma=False
    )
```

profile of v0, /device:TPU:0, one launch (start us, length us, event | category | flops | bytes accessed | tf_op | source)
XLA Modules:
  0.0 1144.2 jit_solution(3510027396027910421)
XLA Ops:
  20.4 197.7 %while.80 = (s32[]{:T(128)}, f32[8,128,256]{2,1,0:T(8,128)S(1)}, f32[2,64,8,256]{3,1,0,2:T(8,128)}, f32[2,8,128,128]{3,2,1,0:T(8,128)}, f32[2,8,128,128]{3,2,1,0...) while((s32[]{:T(128)}, f32[8,128,256]{2,1,0:T(8,128)S(1)}, ...), condition=%wide.region_2.3_spmd.clone.clone, body=%wide.region_1.2_spmd.clone.clone.sunk | while | flops 2117148800 | bytes 125245144 | solution.py:64
  24.2 80.0 %custom-call.34 = f32[8,1,128,128]{2,3,1,0:T(8,128)} custom-call(f32[8,1,128,128]{3,2,1,0:T(8,128)} %add_bitcast_fusion.5), custom_call_target="InvertDiagBlocksLowerTriangular" | custom-call | tf_op jit(solution)/shard_map/jvp()/while/body/eval_jaxpr/jit(_solve_triangular)/vmap()/triangular_solve | solution.py:37
  122.9 80.0 %custom-call.34 = f32[8,1,128,128]{2,3,1,0:T(8,128)} custom-call(f32[8,1,128,128]{3,2,1,0:T(8,128)} %add_bitcast_fusion.5), custom_call_target="InvertDiagBlocksLowerTriangular" | custom-call | tf_op jit(solution)/shard_map/jvp()/while/body/eval_jaxpr/jit(_solve_triangular)/vmap()/triangular_solve | solution.py:37
  219.4 246.9 %while.77 = (s32[]{:T(128)}, f32[8,128,128]{2,1,0:T(8,128)S(1)}, f32[8,128,128]{2,1,0:T(8,128)}, f32[8,128,128]{2,1,0:T(8,128)}, s32[]{:T(128)}) while((s32[]{:T(128)}, f32[8,128,128]{2,1,0:T(8,128)S(1)}, f32[8,128,128]{2,1,0:T(8,128)}, f32[8,128,128]{2,1,0:T(8,128)}, s32[]{:T(128)}) %tuple.145), condition=%wide.region_4.5_spmd, body=%wide.region_3.4_spmd.sunk | while | flops 201457664 | bytes 4194405 | solution.py:106
  221.2 3.9 collective-permute-start
  225.2 11.1 collective-permute-done
  238.2 4.4 collective-permute-start
  242.6 10.3 collective-permute-done
  254.7 4.4 collective-permute-start
  259.1 9.3 collective-permute-done
  270.3 4.4 collective-permute-start
  274.8 8.4 collective-permute-done
  285.0 4.4 collective-permute-start
  289.5 7.5 collective-permute-done
  298.8 5.3 collective-permute-start
  304.2 6.7 collective-permute-done
  312.7 6.5 collective-permute-start
  319.2 6.6 collective-permute-done
  327.7 6.5 collective-permute-start
  334.2 6.6 collective-permute-done
  342.7 6.5 collective-permute-start
  349.3 6.6 collective-permute-done
  357.8 6.7 collective-permute-start
  364.4 7.6 collective-permute-done
  373.9 7.1 collective-permute-start
  381.0 8.6 collective-permute-done
  391.5 7.4 collective-permute-start
  398.9 9.7 collective-permute-done
  410.5 7.4 collective-permute-start
  417.9 10.8 collective-permute-done
  430.6 7.5 collective-permute-start
  438.1 12.0 %collective-permute-done = f32[8,128,128]{2,1,0:T(8,128)S(1)} collective-permute-done((f32[8,128,128]{2,1,0:T(8,128)S(1)}, f32[8,128,128]{2,1,0:T(8,128)S(1)}, u32[]{:S(2)}, u32[]{:S(2)}) %collective-permute-start) | collective-permute-done | bytes 524320 | tf_op jit(solution)/shard_map/while/body/eval_jaxpr/ppermute | solution.py:18
  451.9 7.3 collective-permute-start
  459.3 6.6 collective-permute-done
  468.5 4.5 fusion.106
  476.6 2.7 mul.255
  479.3 3.5 fusion.104
  484.7 282.4 %while.78 = (s32[]{:T(128)}, f32[8,128,128]{2,1,0:T(8,128)S(1)}, f32[8,128,128]{2,1,0:T(8,128)}, f32[8,128,128]{2,1,0:T(8,128)S(1)}, s32[]{:T(128)}) while((s32[]{:T(128)}, f32[8,128,128]{2,1,0:T(8,128)S(1)}, f32[8,128,128]{2,1,0:T(8,128)}, f32[8,128,128]{2,1,0:T(8,128)S(1)}, s32[]{:T(128)}) %tuple.148), condition=%wide.region_6.7_spmd, body=%wide.region_5.6_spmd.sunk | while | flops 201457664 | bytes 4194405 | solution.py:130
  488.5 20.5 %collective-permute-done.1 = f32[8,128,128]{2,1,0:T(8,128)S(1)} collective-permute-done((f32[8,128,128]{2,1,0:T(8,128)}, f32[8,128,128]{2,1,0:T(8,128)S(1)}, u32[]{:S(2)}, u32[]{:S(2)}) %collective-permute-start.1) | collective-permute-done | bytes 524320 | tf_op jit(solution)/shard_map/while/body/eval_jaxpr/ppermute | solution.py:18
  512.8 18.8 %collective-permute-done.1 = f32[8,128,128]{2,1,0:T(8,128)S(1)} collective-permute-done((f32[8,128,128]{2,1,0:T(8,128)}, f32[8,128,128]{2,1,0:T(8,128)S(1)}, u32[]{:S(2)}, u32[]{:S(2)}) %collective-permute-start.1) | collective-permute-done | bytes 524320 | tf_op jit(solution)/shard_map/while/body/eval_jaxpr/ppermute | solution.py:18
  535.4 17.8 %collective-permute-done.1 = f32[8,128,128]{2,1,0:T(8,128)S(1)} collective-permute-done((f32[8,128,128]{2,1,0:T(8,128)}, f32[8,128,128]{2,1,0:T(8,128)S(1)}, u32[]{:S(2)}, u32[]{:S(2)}) %collective-permute-start.1) | collective-permute-done | bytes 524320 | tf_op jit(solution)/shard_map/while/body/eval_jaxpr/ppermute | solution.py:18
  557.0 15.2 %collective-permute-done.1 = f32[8,128,128]{2,1,0:T(8,128)S(1)} collective-permute-done((f32[8,128,128]{2,1,0:T(8,128)}, f32[8,128,128]{2,1,0:T(8,128)S(1)}, u32[]{:S(2)}, u32[]{:S(2)}) %collective-permute-start.1) | collective-permute-done | bytes 524320 | tf_op jit(solution)/shard_map/while/body/eval_jaxpr/ppermute | solution.py:18
  575.9 14.5 %collective-permute-done.1 = f32[8,128,128]{2,1,0:T(8,128)S(1)} collective-permute-done((f32[8,128,128]{2,1,0:T(8,128)}, f32[8,128,128]{2,1,0:T(8,128)S(1)}, u32[]{:S(2)}, u32[]{:S(2)}) %collective-permute-start.1) | collective-permute-done | bytes 524320 | tf_op jit(solution)/shard_map/while/body/eval_jaxpr/ppermute | solution.py:18
  594.3 14.8 %collective-permute-done.1 = f32[8,128,128]{2,1,0:T(8,128)S(1)} collective-permute-done((f32[8,128,128]{2,1,0:T(8,128)}, f32[8,128,128]{2,1,0:T(8,128)S(1)}, u32[]{:S(2)}, u32[]{:S(2)}) %collective-permute-start.1) | collective-permute-done | bytes 524320 | tf_op jit(solution)/shard_map/while/body/eval_jaxpr/ppermute | solution.py:18
  612.9 11.4 collective-permute-done.1
  628.1 13.1 %collective-permute-done.1 = f32[8,128,128]{2,1,0:T(8,128)S(1)} collective-permute-done((f32[8,128,128]{2,1,0:T(8,128)}, f32[8,128,128]{2,1,0:T(8,128)S(1)}, u32[]{:S(2)}, u32[]{:S(2)}) %collective-permute-start.1) | collective-permute-done | bytes 524320 | tf_op jit(solution)/shard_map/while/body/eval_jaxpr/ppermute | solution.py:18
  644.9 11.8 %collective-permute-done.1 = f32[8,128,128]{2,1,0:T(8,128)S(1)} collective-permute-done((f32[8,128,128]{2,1,0:T(8,128)}, f32[8,128,128]{2,1,0:T(8,128)S(1)}, u32[]{:S(2)}, u32[]{:S(2)}) %collective-permute-start.1) | collective-permute-done | bytes 524320 | tf_op jit(solution)/shard_map/while/body/eval_jaxpr/ppermute | solution.py:18
  660.5 12.9 %collective-permute-done.1 = f32[8,128,128]{2,1,0:T(8,128)S(1)} collective-permute-done((f32[8,128,128]{2,1,0:T(8,128)}, f32[8,128,128]{2,1,0:T(8,128)S(1)}, u32[]{:S(2)}, u32[]{:S(2)}) %collective-permute-start.1) | collective-permute-done | bytes 524320 | tf_op jit(solution)/shard_map/while/body/eval_jaxpr/ppermute | solution.py:18
  677.2 14.7 %collective-permute-done.1 = f32[8,128,128]{2,1,0:T(8,128)S(1)} collective-permute-done((f32[8,128,128]{2,1,0:T(8,128)}, f32[8,128,128]{2,1,0:T(8,128)S(1)}, u32[]{:S(2)}, u32[]{:S(2)}) %collective-permute-start.1) | collective-permute-done | bytes 524320 | tf_op jit(solution)/shard_map/while/body/eval_jaxpr/ppermute | solution.py:18
  695.7 16.1 %collective-permute-done.1 = f32[8,128,128]{2,1,0:T(8,128)S(1)} collective-permute-done((f32[8,128,128]{2,1,0:T(8,128)}, f32[8,128,128]{2,1,0:T(8,128)S(1)}, u32[]{:S(2)}, u32[]{:S(2)}) %collective-permute-start.1) | collective-permute-done | bytes 524320 | tf_op jit(solution)/shard_map/while/body/eval_jaxpr/ppermute | solution.py:18
  715.6 16.2 %collective-permute-done.1 = f32[8,128,128]{2,1,0:T(8,128)S(1)} collective-permute-done((f32[8,128,128]{2,1,0:T(8,128)}, f32[8,128,128]{2,1,0:T(8,128)S(1)}, u32[]{:S(2)}, u32[]{:S(2)}) %collective-permute-start.1) | collective-permute-done | bytes 524320 | tf_op jit(solution)/shard_map/while/body/eval_jaxpr/ppermute | solution.py:18
  735.6 14.2 %collective-permute-done.1 = f32[8,128,128]{2,1,0:T(8,128)S(1)} collective-permute-done((f32[8,128,128]{2,1,0:T(8,128)}, f32[8,128,128]{2,1,0:T(8,128)S(1)}, u32[]{:S(2)}, u32[]{:S(2)}) %collective-permute-start.1) | collective-permute-done | bytes 524320 | tf_op jit(solution)/shard_map/while/body/eval_jaxpr/ppermute | solution.py:18
  753.6 13.5 %collective-permute-done.1 = f32[8,128,128]{2,1,0:T(8,128)S(1)} collective-permute-done((f32[8,128,128]{2,1,0:T(8,128)}, f32[8,128,128]{2,1,0:T(8,128)S(1)}, u32[]{:S(2)}, u32[]{:S(2)}) %collective-permute-start.1) | collective-permute-done | bytes 524320 | tf_op jit(solution)/shard_map/while/body/eval_jaxpr/ppermute | solution.py:18
  782.4 240.7 %while.79 = (s32[]{:T(128)}, f32[8,128,256]{2,1,0:T(8,128)S(1)}, bf16[2,64,8,128]{3,1,2,0:T(8,128)(2,1)}, f32[2,128,8,128]{3,1,2,0:T(8,128)}, bf16[2,128,8,256]{...) while((s32[]{:T(128)}, f32[8,128,256]{2,1,0:T(8,128)S(1)}, ...), condition=%wide.region_10.11_spmd.clone, body=%wide.region_7.10_spmd.clone.sunk | while | flops 4434402304 | bytes 127030184 | solution.py:64
  788.8 3.0 fusion.215
  791.9 79.2 %custom-call.33 = f32[8,1,128,128]{2,3,1,0:T(8,128)} custom-call(f32[8,1,128,128]{3,2,1,0:T(8,128)S(1)} %add_bitcast_fusion.4), custom_call_target="InvertDiagBlocksLowerTriangular" | custom-call | tf_op jit(solution)/shard_map/transpose(jvp())/while/body/eval_jaxpr/jit(_solve_triangular)/vmap()/triangular_solve | solution.py:37
  877.0 3.4 fusion.213
  883.7 3.1 fusion.214
  908.9 3.0 fusion.215
  912.0 79.2 %custom-call.33 = f32[8,1,128,128]{2,3,1,0:T(8,128)} custom-call(f32[8,1,128,128]{3,2,1,0:T(8,128)S(1)} %add_bitcast_fusion.4), custom_call_target="InvertDiagBlocksLowerTriangular" | custom-call | tf_op jit(solution)/shard_map/transpose(jvp())/while/body/eval_jaxpr/jit(_solve_triangular)/vmap()/triangular_solve | solution.py:37
  997.1 3.4 fusion.213
  1003.9 3.1 fusion.214
  1032.8 3.9 fusion.100
  1038.5 98.6 %reduce-scatter.2.cloned.1.call-done = f32[8,2048]{1,0:T(8,128)} async-done(((f32[1024,2048]{1,0:T(8,128)}), f32[8,2048]{1,0:T(8,128)}) %reduce-scatter.2.cloned.1.call-update) | async-done | bytes 65552 | tf_op jit(solution)/shard_map/reduce_scatter | solution.py:136
  (374 shorter events, 231.8 us)
Async XLA Ops:
  7.2 461.4 %copy-start = (bf16[1,128,2048]{2,1,0:T(8,128)(2,1)S(1)}, bf16[1,128,2048]{2,1,0:T(8,128)(2,1)}, u32[]{:S(2)}) copy-start(bf16[1,128,2048]{2,1,0:T(8,128)(2,1)} %param.18) | copy-start | bytes 1572868
  7.2 472.1 %all-gather.2.cloned.1.call-start = ((), (), s32[]{:S(2)}) async-start(), calls=%async_computation.1 | async-start | bytes 4227072 | tf_op jit(solution)/shard_map/all_gather | solution.py:114
  7.9 1129.2 %reduce-scatter.2.cloned.1.call-start = ((), (), s32[]{:S(2)}) async-start(), calls=%async_computation.2 | async-start | bytes 8454144 | tf_op jit(solution)/shard_map/reduce_scatter | solution.py:136
  9.4 10.5 copy-start.22
  109.4 3.7 copy-start.10
  109.4 3.0 copy-start.45
  208.1 3.7 copy-start.10
  208.1 3.0 copy-start.45
  221.2 15.1 %collective-permute-start = (f32[8,128,128]{2,1,0:T(8,128)S(1)}, f32[8,128,128]{2,1,0:T(8,128)S(1)}, u32[]{:S(2)}, u32[]{:S(2)}) collective-permute-start(f32[8,128,128]{2,1,0:T(8,128)S(1)} %convolution_add_fusion.17), channel_id=1, source_target_pairs={{0,1},{1,2},{2,3},{3,4},{4,5},{5,6},{6,7},{7,8},{8,9},{9,10},{10,1... | collective-permute-start | bytes 1572872 | tf_op jit(solution)/shard_map/while/body/eval_jaxpr/ppermute | solution.py:18
  238.2 14.7 %collective-permute-start = (f32[8,128,128]{2,1,0:T(8,128)S(1)}, f32[8,128,128]{2,1,0:T(8,128)S(1)}, u32[]{:S(2)}, u32[]{:S(2)}) collective-permute-start(f32[8,128,128]{2,1,0:T(8,128)S(1)} %convolution_add_fusion.17), channel_id=1, source_target_pairs={{0,1},{1,2},{2,3},{3,4},{4,5},{5,6},{6,7},{7,8},{8,9},{9,10},{10,1... | collective-permute-start | bytes 1572872 | tf_op jit(solution)/shard_map/while/body/eval_jaxpr/ppermute | solution.py:18
  254.7 13.8 %collective-permute-start = (f32[8,128,128]{2,1,0:T(8,128)S(1)}, f32[8,128,128]{2,1,0:T(8,128)S(1)}, u32[]{:S(2)}, u32[]{:S(2)}) collective-permute-start(f32[8,128,128]{2,1,0:T(8,128)S(1)} %convolution_add_fusion.17), channel_id=1, source_target_pairs={{0,1},{1,2},{2,3},{3,4},{4,5},{5,6},{6,7},{7,8},{8,9},{9,10},{10,1... | collective-permute-start | bytes 1572872 | tf_op jit(solution)/shard_map/while/body/eval_jaxpr/ppermute | solution.py:18
  270.3 12.8 %collective-permute-start = (f32[8,128,128]{2,1,0:T(8,128)S(1)}, f32[8,128,128]{2,1,0:T(8,128)S(1)}, u32[]{:S(2)}, u32[]{:S(2)}) collective-permute-start(f32[8,128,128]{2,1,0:T(8,128)S(1)} %convolution_add_fusion.17), channel_id=1, source_target_pairs={{0,1},{1,2},{2,3},{3,4},{4,5},{5,6},{6,7},{7,8},{8,9},{9,10},{10,1... | collective-permute-start | bytes 1572872 | tf_op jit(solution)/shard_map/while/body/eval_jaxpr/ppermute | solution.py:18
  285.0 11.9 %collective-permute-start = (f32[8,128,128]{2,1,0:T(8,128)S(1)}, f32[8,128,128]{2,1,0:T(8,128)S(1)}, u32[]{:S(2)}, u32[]{:S(2)}) collective-permute-start(f32[8,128,128]{2,1,0:T(8,128)S(1)} %convolution_add_fusion.17), channel_id=1, source_target_pairs={{0,1},{1,2},{2,3},{3,4},{4,5},{5,6},{6,7},{7,8},{8,9},{9,10},{10,1... | collective-permute-start | bytes 1572872 | tf_op jit(solution)/shard_map/while/body/eval_jaxpr/ppermute | solution.py:18
  298.8 12.0 %collective-permute-start = (f32[8,128,128]{2,1,0:T(8,128)S(1)}, f32[8,128,128]{2,1,0:T(8,128)S(1)}, u32[]{:S(2)}, u32[]{:S(2)}) collective-permute-start(f32[8,128,128]{2,1,0:T(8,128)S(1)} %convolution_add_fusion.17), channel_id=1, source_target_pairs={{0,1},{1,2},{2,3},{3,4},{4,5},{5,6},{6,7},{7,8},{8,9},{9,10},{10,1... | collective-permute-start | bytes 1572872 | tf_op jit(solution)/shard_map/while/body/eval_jaxpr/ppermute | solution.py:18
  312.7 13.2 %collective-permute-start = (f32[8,128,128]{2,1,0:T(8,128)S(1)}, f32[8,128,128]{2,1,0:T(8,128)S(1)}, u32[]{:S(2)}, u32[]{:S(2)}) collective-permute-start(f32[8,128,128]{2,1,0:T(8,128)S(1)} %convolution_add_fusion.17), channel_id=1, source_target_pairs={{0,1},{1,2},{2,3},{3,4},{4,5},{5,6},{6,7},{7,8},{8,9},{9,10},{10,1... | collective-permute-start | bytes 1572872 | tf_op jit(solution)/shard_map/while/body/eval_jaxpr/ppermute | solution.py:18
  327.7 13.2 %collective-permute-start = (f32[8,128,128]{2,1,0:T(8,128)S(1)}, f32[8,128,128]{2,1,0:T(8,128)S(1)}, u32[]{:S(2)}, u32[]{:S(2)}) collective-permute-start(f32[8,128,128]{2,1,0:T(8,128)S(1)} %convolution_add_fusion.17), channel_id=1, source_target_pairs={{0,1},{1,2},{2,3},{3,4},{4,5},{5,6},{6,7},{7,8},{8,9},{9,10},{10,1... | collective-permute-start | bytes 1572872 | tf_op jit(solution)/shard_map/while/body/eval_jaxpr/ppermute | solution.py:18
  342.7 13.2 %collective-permute-start = (f32[8,128,128]{2,1,0:T(8,128)S(1)}, f32[8,128,128]{2,1,0:T(8,128)S(1)}, u32[]{:S(2)}, u32[]{:S(2)}) collective-permute-start(f32[8,128,128]{2,1,0:T(8,128)S(1)} %convolution_add_fusion.17), channel_id=1, source_target_pairs={{0,1},{1,2},{2,3},{3,4},{4,5},{5,6},{6,7},{7,8},{8,9},{9,10},{10,1... | collective-permute-start | bytes 1572872 | tf_op jit(solution)/shard_map/while/body/eval_jaxpr/ppermute | solution.py:18
  357.8 14.2 %collective-permute-start = (f32[8,128,128]{2,1,0:T(8,128)S(1)}, f32[8,128,128]{2,1,0:T(8,128)S(1)}, u32[]{:S(2)}, u32[]{:S(2)}) collective-permute-start(f32[8,128,128]{2,1,0:T(8,128)S(1)} %convolution_add_fusion.17), channel_id=1, source_target_pairs={{0,1},{1,2},{2,3},{3,4},{4,5},{5,6},{6,7},{7,8},{8,9},{9,10},{10,1... | collective-permute-start | bytes 1572872 | tf_op jit(solution)/shard_map/while/body/eval_jaxpr/ppermute | solution.py:18
  373.9 15.8 %collective-permute-start = (f32[8,128,128]{2,1,0:T(8,128)S(1)}, f32[8,128,128]{2,1,0:T(8,128)S(1)}, u32[]{:S(2)}, u32[]{:S(2)}) collective-permute-start(f32[8,128,128]{2,1,0:T(8,128)S(1)} %convolution_add_fusion.17), channel_id=1, source_target_pairs={{0,1},{1,2},{2,3},{3,4},{4,5},{5,6},{6,7},{7,8},{8,9},{9,10},{10,1... | collective-permute-start | bytes 1572872 | tf_op jit(solution)/shard_map/while/body/eval_jaxpr/ppermute | solution.py:18
  391.5 17.2 %collective-permute-start = (f32[8,128,128]{2,1,0:T(8,128)S(1)}, f32[8,128,128]{2,1,0:T(8,128)S(1)}, u32[]{:S(2)}, u32[]{:S(2)}) collective-permute-start(f32[8,128,128]{2,1,0:T(8,128)S(1)} %convolution_add_fusion.17), channel_id=1, source_target_pairs={{0,1},{1,2},{2,3},{3,4},{4,5},{5,6},{6,7},{7,8},{8,9},{9,10},{10,1... | collective-permute-start | bytes 1572872 | tf_op jit(solution)/shard_map/while/body/eval_jaxpr/ppermute | solution.py:18
  410.5 18.3 %collective-permute-start = (f32[8,128,128]{2,1,0:T(8,128)S(1)}, f32[8,128,128]{2,1,0:T(8,128)S(1)}, u32[]{:S(2)}, u32[]{:S(2)}) collective-permute-start(f32[8,128,128]{2,1,0:T(8,128)S(1)} %convolution_add_fusion.17), channel_id=1, source_target_pairs={{0,1},{1,2},{2,3},{3,4},{4,5},{5,6},{6,7},{7,8},{8,9},{9,10},{10,1... | collective-permute-start | bytes 1572872 | tf_op jit(solution)/shard_map/while/body/eval_jaxpr/ppermute | solution.py:18
  430.6 19.5 %collective-permute-start = (f32[8,128,128]{2,1,0:T(8,128)S(1)}, f32[8,128,128]{2,1,0:T(8,128)S(1)}, u32[]{:S(2)}, u32[]{:S(2)}) collective-permute-start(f32[8,128,128]{2,1,0:T(8,128)S(1)} %convolution_add_fusion.17), channel_id=1, source_target_pairs={{0,1},{1,2},{2,3},{3,4},{4,5},{5,6},{6,7},{7,8},{8,9},{9,10},{10,1... | collective-permute-start | bytes 1572872 | tf_op jit(solution)/shard_map/while/body/eval_jaxpr/ppermute | solution.py:18
  451.9 14.0 %collective-permute-start = (f32[8,128,128]{2,1,0:T(8,128)S(1)}, f32[8,128,128]{2,1,0:T(8,128)S(1)}, u32[]{:S(2)}, u32[]{:S(2)}) collective-permute-start(f32[8,128,128]{2,1,0:T(8,128)S(1)} %convolution_add_fusion.17), channel_id=1, source_target_pairs={{0,1},{1,2},{2,3},{3,4},{4,5},{5,6},{6,7},{7,8},{8,9},{9,10},{10,1... | collective-permute-start | bytes 1572872 | tf_op jit(solution)/shard_map/while/body/eval_jaxpr/ppermute | solution.py:18
  466.3 301.8 %copy-start.13 = (f32[8,128,128]{2,1,0:T(8,128)}, f32[8,128,128]{2,1,0:T(8,128)S(1)}, u32[]{:S(2)}) copy-start(f32[8,128,128]{2,1,0:T(8,128)S(1)} %get-tuple-element.596) | copy-start | bytes 1572868
  468.5 4.6 copy-start.39
  479.3 4.3 copy-start.47
  487.2 21.8 %collective-permute-start.1 = (f32[8,128,128]{2,1,0:T(8,128)}, f32[8,128,128]{2,1,0:T(8,128)S(1)}, u32[]{:S(2)}, u32[]{:S(2)}) collective-permute-start(f32[8,128,128]{2,1,0:T(8,128)} %convolution_add_fusion.18), channel_id=1, source_target_pairs={{1,0},{2,1},{3,2},{4,3},{5,4},{6,5},{7,6},{8,7},{9,8},{10,9},{11,1... | collective-permute-start | bytes 1572872 | tf_op jit(solution)/shard_map/while/body/eval_jaxpr/ppermute | solution.py:18
  511.5 20.1 %collective-permute-start.1 = (f32[8,128,128]{2,1,0:T(8,128)}, f32[8,128,128]{2,1,0:T(8,128)S(1)}, u32[]{:S(2)}, u32[]{:S(2)}) collective-permute-start(f32[8,128,128]{2,1,0:T(8,128)} %convolution_add_fusion.18), channel_id=1, source_target_pairs={{1,0},{2,1},{3,2},{4,3},{5,4},{6,5},{7,6},{8,7},{9,8},{10,9},{11,1... | collective-permute-start | bytes 1572872 | tf_op jit(solution)/shard_map/while/body/eval_jaxpr/ppermute | solution.py:18
  534.1 19.1 %collective-permute-start.1 = (f32[8,128,128]{2,1,0:T(8,128)}, f32[8,128,128]{2,1,0:T(8,128)S(1)}, u32[]{:S(2)}, u32[]{:S(2)}) collective-permute-start(f32[8,128,128]{2,1,0:T(8,128)} %convolution_add_fusion.18), channel_id=1, source_target_pairs={{1,0},{2,1},{3,2},{4,3},{5,4},{6,5},{7,6},{8,7},{9,8},{10,9},{11,1... | collective-permute-start | bytes 1572872 | tf_op jit(solution)/shard_map/while/body/eval_jaxpr/ppermute | solution.py:18
  555.7 16.4 %collective-permute-start.1 = (f32[8,128,128]{2,1,0:T(8,128)}, f32[8,128,128]{2,1,0:T(8,128)S(1)}, u32[]{:S(2)}, u32[]{:S(2)}) collective-permute-start(f32[8,128,128]{2,1,0:T(8,128)} %convolution_add_fusion.18), channel_id=1, source_target_pairs={{1,0},{2,1},{3,2},{4,3},{5,4},{6,5},{7,6},{8,7},{9,8},{10,9},{11,1... | collective-permute-start | bytes 1572872 | tf_op jit(solution)/shard_map/while/body/eval_jaxpr/ppermute | solution.py:18
  574.6 15.8 %collective-permute-start.1 = (f32[8,128,128]{2,1,0:T(8,128)}, f32[8,128,128]{2,1,0:T(8,128)S(1)}, u32[]{:S(2)}, u32[]{:S(2)}) collective-permute-start(f32[8,128,128]{2,1,0:T(8,128)} %convolution_add_fusion.18), channel_id=1, source_target_pairs={{1,0},{2,1},{3,2},{4,3},{5,4},{6,5},{7,6},{8,7},{9,8},{10,9},{11,1... | collective-permute-start | bytes 1572872 | tf_op jit(solution)/shard_map/while/body/eval_jaxpr/ppermute | solution.py:18
  593.0 16.1 %collective-permute-start.1 = (f32[8,128,128]{2,1,0:T(8,128)}, f32[8,128,128]{2,1,0:T(8,128)S(1)}, u32[]{:S(2)}, u32[]{:S(2)}) collective-permute-start(f32[8,128,128]{2,1,0:T(8,128)} %convolution_add_fusion.18), channel_id=1, source_target_pairs={{1,0},{2,1},{3,2},{4,3},{5,4},{6,5},{7,6},{8,7},{9,8},{10,9},{11,1... | collective-permute-start | bytes 1572872 | tf_op jit(solution)/shard_map/while/body/eval_jaxpr/ppermute | solution.py:18
  611.6 12.7 %collective-permute-start.1 = (f32[8,128,128]{2,1,0:T(8,128)}, f32[8,128,128]{2,1,0:T(8,128)S(1)}, u32[]{:S(2)}, u32[]{:S(2)}) collective-permute-start(f32[8,128,128]{2,1,0:T(8,128)} %convolution_add_fusion.18), channel_id=1, source_target_pairs={{1,0},{2,1},{3,2},{4,3},{5,4},{6,5},{7,6},{8,7},{9,8},{10,9},{11,1... | collective-permute-start | bytes 1572872 | tf_op jit(solution)/shard_map/while/body/eval_jaxpr/ppermute | solution.py:18
  626.8 14.4 %collective-permute-start.1 = (f32[8,128,128]{2,1,0:T(8,128)}, f32[8,128,128]{2,1,0:T(8,128)S(1)}, u32[]{:S(2)}, u32[]{:S(2)}) collective-permute-start(f32[8,128,128]{2,1,0:T(8,128)} %convolution_add_fusion.18), channel_id=1, source_target_pairs={{1,0},{2,1},{3,2},{4,3},{5,4},{6,5},{7,6},{8,7},{9,8},{10,9},{11,1... | collective-permute-start | bytes 1572872 | tf_op jit(solution)/shard_map/while/body/eval_jaxpr/ppermute | solution.py:18
  643.6 13.1 %collective-permute-start.1 = (f32[8,128,128]{2,1,0:T(8,128)}, f32[8,128,128]{2,1,0:T(8,128)S(1)}, u32[]{:S(2)}, u32[]{:S(2)}) collective-permute-start(f32[8,128,128]{2,1,0:T(8,128)} %convolution_add_fusion.18), channel_id=1, source_target_pairs={{1,0},{2,1},{3,2},{4,3},{5,4},{6,5},{7,6},{8,7},{9,8},{10,9},{11,1... | collective-permute-start | bytes 1572872 | tf_op jit(solution)/shard_map/while/body/eval_jaxpr/ppermute | solution.py:18
  659.3 14.2 %collective-permute-start.1 = (f32[8,128,128]{2,1,0:T(8,128)}, f32[8,128,128]{2,1,0:T(8,128)S(1)}, u32[]{:S(2)}, u32[]{:S(2)}) collective-permute-start(f32[8,128,128]{2,1,0:T(8,128)} %convolution_add_fusion.18), channel_id=1, source_target_pairs={{1,0},{2,1},{3,2},{4,3},{5,4},{6,5},{7,6},{8,7},{9,8},{10,9},{11,1... | collective-permute-start | bytes 1572872 | tf_op jit(solution)/shard_map/while/body/eval_jaxpr/ppermute | solution.py:18
  675.9 16.0 %collective-permute-start.1 = (f32[8,128,128]{2,1,0:T(8,128)}, f32[8,128,128]{2,1,0:T(8,128)S(1)}, u32[]{:S(2)}, u32[]{:S(2)}) collective-permute-start(f32[8,128,128]{2,1,0:T(8,128)} %convolution_add_fusion.18), channel_id=1, source_target_pairs={{1,0},{2,1},{3,2},{4,3},{5,4},{6,5},{7,6},{8,7},{9,8},{10,9},{11,1... | collective-permute-start | bytes 1572872 | tf_op jit(solution)/shard_map/while/body/eval_jaxpr/ppermute | solution.py:18
  694.4 17.4 %collective-permute-start.1 = (f32[8,128,128]{2,1,0:T(8,128)}, f32[8,128,128]{2,1,0:T(8,128)S(1)}, u32[]{:S(2)}, u32[]{:S(2)}) collective-permute-start(f32[8,128,128]{2,1,0:T(8,128)} %convolution_add_fusion.18), channel_id=1, source_target_pairs={{1,0},{2,1},{3,2},{4,3},{5,4},{6,5},{7,6},{8,7},{9,8},{10,9},{11,1... | collective-permute-start | bytes 1572872 | tf_op jit(solution)/shard_map/while/body/eval_jaxpr/ppermute | solution.py:18
  714.3 17.5 %collective-permute-start.1 = (f32[8,128,128]{2,1,0:T(8,128)}, f32[8,128,128]{2,1,0:T(8,128)S(1)}, u32[]{:S(2)}, u32[]{:S(2)}) collective-permute-start(f32[8,128,128]{2,1,0:T(8,128)} %convolution_add_fusion.18), channel_id=1, source_target_pairs={{1,0},{2,1},{3,2},{4,3},{5,4},{6,5},{7,6},{8,7},{9,8},{10,9},{11,1... | collective-permute-start | bytes 1572872 | tf_op jit(solution)/shard_map/while/body/eval_jaxpr/ppermute | solution.py:18
  734.3 15.5 %collective-permute-start.1 = (f32[8,128,128]{2,1,0:T(8,128)}, f32[8,128,128]{2,1,0:T(8,128)S(1)}, u32[]{:S(2)}, u32[]{:S(2)}) collective-permute-start(f32[8,128,128]{2,1,0:T(8,128)} %convolution_add_fusion.18), channel_id=1, source_target_pairs={{1,0},{2,1},{3,2},{4,3},{5,4},{6,5},{7,6},{8,7},{9,8},{10,9},{11,1... | collective-permute-start | bytes 1572872 | tf_op jit(solution)/shard_map/while/body/eval_jaxpr/ppermute | solution.py:18
  752.4 14.8 %collective-permute-start.1 = (f32[8,128,128]{2,1,0:T(8,128)}, f32[8,128,128]{2,1,0:T(8,128)S(1)}, u32[]{:S(2)}, u32[]{:S(2)}) collective-permute-start(f32[8,128,128]{2,1,0:T(8,128)} %convolution_add_fusion.18), channel_id=1, source_target_pairs={{1,0},{2,1},{3,2},{4,3},{5,4},{6,5},{7,6},{8,7},{9,8},{10,9},{11,1... | collective-permute-start | bytes 1572872 | tf_op jit(solution)/shard_map/while/body/eval_jaxpr/ppermute | solution.py:18
  769.3 3.7 copy-start.14
  782.5 3.0 copy-start.7
  784.5 4.3 copy-start.19
  788.0 3.9 copy-start.28
  877.0 3.5 copy-start.11
  880.4 6.5 copy-start.6
  893.7 3.1 copy-start.31
  894.0 4.8 copy-start.42
  898.8 3.9 copy-start.3
  902.7 3.0 copy-start.7
  904.6 4.3 copy-start.19
  908.1 3.9 copy-start.28
  997.1 3.5 copy-start.11
  1000.6 6.5 copy-start.6
  1013.8 3.1 copy-start.31
  1014.2 4.8 copy-start.42
  1019.0 3.9 copy-start.3
  1028.9 3.8 copy-start.40
  1032.8 3.9 copy-start.32
  1032.8 3.9 copy-start.33
  1032.8 3.9 copy-start.34
  1032.8 3.9 copy-start.35
  1032.8 104.3 %copy-start.1 = (bf16[1,128,2048]{2,1,0:T(8,128)(2,1)S(1)}, bf16[1,128,2048]{2,1,0:T(8,128)(2,1)}, u32[]{:S(2)}) copy-start(bf16[1,128,2048]{2,1,0:T(8,128)(2,1)} %param.18) | copy-start | bytes 1572868
  (49 other events, 88.6 us)
Sparse Core Ops, SparseCore 0:
  11.2 69.7 all-gather.1
  473.2 663.8 reduce-scatter.1
where the time goes:
time: 1150 us; the launch traced here: 1140 us
  waiting for transfers between devices  454 us (39%)
  other arithmetic  333 us (29%)
  matrix products  164 us (14%)
  starting transfers between devices  109 us (9%)
  local copies, waits for them, and re-layouts  67.3 us (6%)
  between operations  14.7 us (1%)
    ppermute x30, waiting for transfers between devices, passed_along(): lax.ppermute(value, axis, [(source, source + steps) for source in range(f...  354 us
    another operation x16, other arithmetic, block_update(): jax.scipy.linalg.solve_triangular(system, beta_heads[:, :, None] * stacke...  321 us
    ppermute x30, starting transfers between devices, passed_along(): lax.ppermute(value, axis, [(source, source + steps) for source in range(f...  109 us
    reduce_scatter x1, waiting for transfers between devices, per_device(): lax.psum_scatter(lax.dot_general(mixed_bf, cot_one, (((0,), (0,)), ((), (...  98.6 us
    dot_general x15, matrix products, pass_adjoint(): jnp.einsum('hdk,hke->hde', flipped, carried, precision=HIGHEST_PREC)  37.4 us
    dot_general x15, matrix products, pass_state(): jnp.einsum('hdk,hke->hde', transit, carried, precision=HIGHEST_PREC)  27.6 us
  transfers between devices with their start and end apart: 32, of which 31 were waited for; matrix products, arithmetic and copies ran while one was open for 48% of the time, Pallas kernels for 0%

commit v1 on v0

v1 whole, which is shorter than its diff:
```python
import jax
import jax.numpy as jnp
from jax import lax
from jax.experimental import pallas as pl
from jax.experimental.pallas import tpu as pltpu
from jax.sharding import PartitionSpec as P

f32, bf16 = jnp.float32, jnp.bfloat16
MESH = pl.DeviceIdType.MESH
NORM_EPS = 1e-06
HEADS = 8
DIM = 128
HALF = 64
FRAMES = 128
STEPS = 256
MODEL = 2048
FEATURES = HEADS * DIM
SEQ = 16
SIDE = 4
COLS = 512


def mm(a, b, ca=1, cb=0):
    return lax.dot_general(a, b, (((ca,), (cb,)), ((), ())), preferred_element_type=f32)


def split(x):
    high = x.astype(bf16)
    return high, (x - high.astype(f32)).astype(bf16)


def mm2(a, b, ca=1, cb=0):
    return mm(a[0], b, ca, cb) + mm(a[1], b, ca, cb)


def mm3(a, b, ca=1, cb=0):
    return mm(a[0], b[0], ca, cb) + (mm(a[0], b[1], ca, cb) + mm(a[1], b[0], ca, cb))


def iota(shape, axis):
    return lax.broadcasted_iota(jnp.int32, shape, axis)


def unit_lower_inverse(blocks):
    shape = blocks[0].shape
    rows, columns = iota(shape, 0), iota(shape, 1)
    differing = rows ^ columns
    eye = (rows == columns).astype(f32)
    inverses = [eye - jnp.where(differing == 1, low, 0.0) for low in blocks]
    size = 2
    while size < shape[0]:
        mask = (differing >= size) & (differing < 2 * size)
        parts = [split(inverse) for inverse in inverses]
        offs = [split(jnp.where(mask, low, 0.0)) for low in blocks]
        firsts = [split(mm3(part, off)) for part, off in zip(parts, offs)]
        inverses = [inv - mm3(first, part) for inv, first, part in zip(inverses, firsts, parts)]
        size *= 2
    return inverses


def pick_column(array, head):
    return jnp.sum(jnp.where(iota(array.shape, 1) == head, array, 0.0), axis=1, keepdims=True)


def row_scale(keys):
    wide = keys.astype(f32)
    return lax.rsqrt(jnp.sum(wide * wide, axis=1, keepdims=True) + NORM_EPS)


def local_forward(heads):
    lows, scales = [], []
    for queries, keys, values, raw_col, raw_row in heads:
        inner = mm(keys, keys, 1, 1)
        rows, columns = iota(inner.shape, 0), iota(inner.shape, 1)
        squares = jnp.sum(jnp.where(rows == columns, inner, 0.0), axis=0, keepdims=True)
        r_row = lax.rsqrt(squares + NORM_EPS)
        r_col = row_scale(keys)
        b_col, b_row = 2.0 * jax.nn.sigmoid(raw_col), 2.0 * jax.nn.sigmoid(raw_row)
        lows.append(jnp.where(columns < rows, inner * (b_col * r_col) * r_row, 0.0))
        scales.append((r_col, r_row, b_col, b_row))
    blocks = []
    for low in lows:
        blocks += [low[:DIM, :DIM], low[DIM:, DIM:]]
    inverses = unit_lower_inverse(blocks)
    results = []
    for index, (queries, keys, values, raw_col, raw_row) in enumerate(heads):
        r_col, r_row, b_col, b_row = scales[index]
        upper, lower = inverses[2 * index], inverses[2 * index + 1]
        corner = mm3(split(lower), split(mm3(split(lows[index][DIM:, :DIM]), split(upper))))
        inverse = jnp.concatenate(
            [
                jnp.concatenate([upper, jnp.zeros_like(upper)], axis=1),
                jnp.concatenate([-corner, lower], axis=1),
            ],
            axis=0,
        )
        written = inverse * b_row
        erase = mm2(split(written * r_row), keys)
        insert = mm2(split(written), values)
        key_back = mm2(split(inverse * r_col), keys, 0, 0)
        scores = mm(queries, keys, 1, 1) * r_row
        frame, step = iota(scores.shape, 0), iota(scores.shape, 1)
        scores = jnp.where(step <= 2 * frame + 1, scores, 0.0)
        score_back = mm3(split(inverse), split(scores), 0, 1)
        eye = (iota((DIM, DIM), 0) == iota((DIM, DIM), 1)).astype(f32)
        erase_scaled = split(erase * r_col)
        transit = eye - (mm(keys, erase_scaled[0], 0, 0) + mm(keys, erase_scaled[1], 0, 0))
        back_scaled = split(key_back * b_col)
        offset = mm(values, back_scaled[0], 0, 0) + mm(values, back_scaled[1], 0, 0)
        weighted = score_back * b_col
        reads = queries.astype(f32) - mm2(split(weighted * r_col), keys, 0, 0)
        mixed = mm2(split(weighted), values, 0, 0)
        results.append((erase, insert, key_back, score_back, transit, offset, reads, mixed, r_row))
    return results


def kernel(
    q_ref, k_ref, v_ref, bcol_ref, brow_ref, cot_ref, w_ref,
    proj_ref, gq_ref, gk_ref, gv_ref, gb_ref, gw_ref,
    wg, wf, cotg, erase_s, insert_s, kback_s, sback_s, reads_s, mixed_s, rrow_s, gm_s, y_s,
    t_send, o_send, z_send, t_recv, o_recv, z_recv,
    s_send, d_send, s_recv, d_recv, mb_send, mb_full, mb_recv, gwp, gwr, gws, gwb,
    w_ss, w_rs, c_ss, c_rs, t_ss, t_rs, o_ss, o_rs, z_ss, z_rs, s_ss, s_rs, d_ss, d_rs,
    m_ss, m_rs, g_ss, g_rs, b_ss, b_rs,
):
    dp, me = lax.axis_index("dp"), lax.axis_index("seq")
    x, c = dp // 2, dp % 2
    y, z = me // SIDE, me % SIDE
    twin = x * 2 + (1 - c)

    def x_peer(step):
        return ((x + step) % SIDE) * 2 + c, me

    def y_peer(step):
        return dp, ((y + step) % SIDE) * SIDE + z

    def z_peer(step):
        return dp, y * SIDE + (z + step) % SIDE

    barrier = pltpu.get_barrier_semaphore()
    for step in range(1, SEQ):
        pl.semaphore_signal(barrier, inc=1, device_id=(dp, (me + step) % SEQ), device_id_type=MESH)
    for step in range(1, SIDE):
        pl.semaphore_signal(barrier, inc=1, device_id=x_peer(step), device_id_type=MESH)
    pl.semaphore_signal(barrier, inc=1, device_id=(twin, me), device_id_type=MESH)
    pl.semaphore_wait(barrier, SEQ - 1 + SIDE - 1 + 1)

    def remote(source, target, send_sem, recv_sem, device):
        return pltpu.make_async_remote_copy(
            src_ref=source, dst_ref=target, send_sem=send_sem, recv_sem=recv_sem,
            device_id=device, device_id_type=MESH,
        )

    def arrival(target, send_sem, recv_sem):
        remote(target, target, send_sem, recv_sem, (twin, me)).wait_recv()

    left, right = pl.ds(0, COLS), pl.ds(COLS, COLS)

    def w_copy(phase, step):
        if phase == 0:
            return wg.at[x, c, y, z], wg.at[(x - step + SIDE) % SIDE, c, y, z], x_peer(step)
        if phase == 1:
            return wg.at[:, c, y, z, :, left], wg.at[:, c, (y - step + SIDE) % SIDE, z, :, left], y_peer(step)
        if phase == 2:
            return wg.at[:, c, y, z, :, right], wg.at[:, c, y, (z - step + SIDE) % SIDE, :, right], z_peer(step)
        if phase == 3:
            return wg.at[:, c, :, z, :, left], wg.at[:, c, :, (z - step + SIDE) % SIDE, :, left], z_peer(step)
        if phase == 4:
            return wg.at[:, c, y, :, :, right], wg.at[:, c, (y - step + SIDE) % SIDE, :, :, right], y_peer(step)
        part = left if step == 1 else right
        return wg.at[:, c, :, :, :, part], wg.at[:, 1 - c, :, :, :, part], (twin, me)

    def w_steps(phase):
        return range(1, 3) if phase == 5 else range(1, SIDE)

    def w_start(phase):
        for step in w_steps(phase):
            source, _, device = w_copy(phase, step)
            sem = 3 * phase + step - 1
            remote(source, source, w_ss.at[sem], w_rs.at[sem], device).start()

    def w_arrive(phase):
        for step in w_steps(phase):
            _, target, _ = w_copy(phase, step)
            sem = 3 * phase + step - 1
            arrival(target, w_ss.at[sem], w_rs.at[sem])

    def w_sent(phase):
        for step in w_steps(phase):
            source, _, device = w_copy(phase, step)
            sem = 3 * phase + step - 1
            remote(source, source, w_ss.at[sem], w_rs.at[sem], device).wait_send()

    wg[x, c, y, z] = w_ref[...]
    w_start(0)

    def cot_copy(step):
        return remote(cot_ref, cotg.at[x], c_ss.at[step - 1], c_rs.at[step - 1], x_peer(step))

    for step in range(1, SIDE):
        cot_copy(step).start()
    cotg[x] = cot_ref[...]

    def head_lanes(head):
        return pl.ds(pl.multiple_of(head * DIM, DIM), DIM)

    def state_copies(head, half):
        owner = 2 * head + half
        rows = pl.ds(half * HALF, HALF)
        return (
            remote(t_send.at[head], t_recv.at[me], t_ss.at[owner], t_rs.at[me], (dp, owner)),
            remote(o_send.at[head, rows], o_recv.at[me], o_ss.at[owner], o_rs.at[me], (dp, owner)),
        )

    def adjoint_copy(head, half):
        owner = 2 * head + half
        rows = pl.ds(half * HALF, HALF)
        return remote(z_send.at[head, rows], z_recv.at[me], z_ss.at[owner], z_rs.at[me], (dp, owner))

    def forward_pair(index, carry):
        pair = (index + y) % SIDE
        heads = []
        for inner in range(2):
            head = 2 * pair + inner
            heads.append(
                (
                    q_ref[:, head_lanes(head)],
                    k_ref[:, head_lanes(head)],
                    v_ref[:, head_lanes(head)],
                    pick_column(bcol_ref[...], head),
                    brow_ref[head],
                )
            )
        for inner, result in enumerate(local_forward(heads)):
            head = 2 * pair + inner
            erase, insert, key_back, score_back, transit, offset, reads, mixed, r_row = result
            t_send[head] = transit
            o_send[head] = offset
            for half in range(2):
                owner = 2 * head + half

                @pl.when(owner != me)
                def _():
                    for copy in state_copies(head, half):
                        copy.start()

                @pl.when(owner == me)
                def _():
                    t_recv[me] = transit
                    o_recv[me] = offset[half * HALF : (half + 1) * HALF]

            erase_s[0, head], erase_s[1, head] = split(erase)
            insert_s[head] = insert
            kback_s[0, head], kback_s[1, head] = split(key_back)
            sback_s[0, head], sback_s[1, head] = split(score_back)
            reads_s[head] = reads.astype(bf16)
            mixed_s[head] = mixed
            rrow_s[head] = r_row

        @pl.when(index == 0)
        def _():
            w_arrive(0)
            w_start(1)
            w_start(2)

        @pl.when(index == 1)
        def _():
            w_arrive(1)
            w_start(3)
            w_arrive(2)
            w_start(4)

        return carry

    lax.fori_loop(0, HEADS // 2, forward_pair, 0)
    w_arrive(3)
    w_arrive(4)
    w_start(5)

    for step in range(1, SEQ):
        source = (me + step) % SEQ
        arrival(t_recv.at[source], t_ss.at[source], t_rs.at[source])
        arrival(o_recv.at[source], o_ss.at[source], o_rs.at[source])

    def send_state(buffer, target, value, segment, send_sems, recv_sems):
        buffer[segment] = value.astype(bf16)

        @pl.when(segment != me)
        def _():
            remote(
                buffer.at[segment], target.at[me], send_sems.at[segment], recv_sems.at[me], (dp, segment)
            ).start()

        @pl.when(segment == me)
        def _():
            target[me] = value.astype(bf16)

    def carry_state(segment, state):
        send_state(s_send, s_recv, state, segment, s_ss, s_rs)
        return mm3(split(state), split(t_recv[segment]), 1, 1) + o_recv[segment]

    last_state = lax.fori_loop(0, SEQ - 1, carry_state, jnp.zeros((HALF, DIM), f32))
    send_state(s_send, s_recv, last_state, SEQ - 1, s_ss, s_rs)

    def order_rows(core):
        def one(index, carry):
            across, block = index // 8, index % 8
            row, column = block // 2, 2 * (block % 2)
            first = wg[across, core, row, column].astype(f32)
            second = wg[across, core, row, column + 1].astype(f32)
            start = pl.multiple_of(((across * 2 + core) * 8 + block) * 16, 16)
            top = jnp.concatenate([first[:8], second[:8]], axis=0)
            bottom = jnp.concatenate([first[8:], second[8:]], axis=0)
            wf[pl.ds(start, 16), pl.ds(0, MODEL // 2)] = top.astype(bf16)
            wf[pl.ds(start, 16), pl.ds(MODEL // 2, MODEL // 2)] = bottom.astype(bf16)
            return carry

        lax.fori_loop(0, 32, one, 0)

    order_rows(c)
    w_arrive(5)
    order_rows(1 - c)

    def gradient_pair(index, carry):
        pair = (index + y) % SIDE
        rows = wf[pl.ds(pl.multiple_of(pair * 2 * DIM, 2 * DIM), 2 * DIM), :]
        both = mm(cot_ref[...], rows, 1, 1).astype(bf16)
        for inner in range(2):
            head = 2 * pair + inner
            grad = both[:, inner * DIM : (inner + 1) * DIM]
            gm_s[head] = grad
            adjoint = mm(grad, reads_s[head], 0, 0).astype(bf16)
            z_send[head] = adjoint
            for half in range(2):
                owner = 2 * head + half

                @pl.when(owner != me)
                def _():
                    adjoint_copy(head, half).start()

                @pl.when(owner == me)
                def _():
                    z_recv[me] = adjoint[half * HALF : (half + 1) * HALF]

        return carry

    lax.fori_loop(0, HEADS // 2, gradient_pair, 0)

    def early_gradient(head, carry):
        y_s[head] = mm2((sback_s[0, head], sback_s[1, head]), gm_s[head])
        return carry

    lax.fori_loop(0, HEADS, early_gradient, 0)

    for step in range(1, SEQ):
        source = (me + step) % SEQ
        arrival(s_recv.at[source], s_ss.at[source], s_rs.at[source])

    def head_state(buffer, head):
        return jnp.concatenate([buffer[2 * head], buffer[2 * head + 1]], axis=0)

    def mix_head(head, carry):
        mixed = (mm(reads_s[head], head_state(s_recv, head), 1, 1) + mixed_s[head]).astype(bf16)
        mb_send[head] = mixed
        mb_full[:, head_lanes(head)] = mixed
        return carry

    lax.fori_loop(0, HEADS, mix_head, 0)

    def mixed_copy(step):
        to = (x + step) % SIDE
        return remote(
            mb_send.at[pl.ds(2 * to, 2)], mb_recv.at[:, x], m_ss.at[step - 1], m_rs.at[step - 1], x_peer(step)
        )

    for step in range(1, SIDE):
        mixed_copy(step).start()
    mb_recv[0, x] = mb_send[2 * x]
    mb_recv[1, x] = mb_send[2 * x + 1]

    for step in range(1, SEQ):
        source = (me + step) % SEQ
        arrival(z_recv.at[source], z_ss.at[source], z_rs.at[source])

    def carry_adjoint(index, state):
        segment = SEQ - 1 - index
        send_state(d_send, d_recv, state, segment, d_ss, d_rs)
        return mm3(split(state), split(t_recv[segment])) + z_recv[segment].astype(f32)

    first_adjoint = lax.fori_loop(0, SEQ - 1, carry_adjoint, jnp.zeros((HALF, DIM), f32))
    send_state(d_send, d_recv, first_adjoint, 0, d_ss, d_rs)

    def project(index, carry):
        lanes = pl.ds(pl.multiple_of(index * COLS, COLS), COLS)
        proj_ref[:, lanes] = mm(mb_full[...], wf[:, lanes]).astype(bf16)
        return carry

    lax.fori_loop(0, MODEL // COLS, project, 0)

    for step in range(1, SIDE):
        source = (x - step + SIDE) % SIDE
        arrival(cotg.at[source], c_ss.at[step - 1], c_rs.at[step - 1])
        arrival(mb_recv.at[:, source], m_ss.at[step - 1], m_rs.at[step - 1])

    def weight_part(inner):
        mixed = mb_recv[inner].reshape(SIDE * FRAMES, DIM)

        def one(index, carry):
            lanes = pl.ds(pl.multiple_of(index * COLS, COLS), COLS)
            cot = cotg[:, :, lanes].reshape(SIDE * FRAMES, COLS)
            gwp[inner, :, lanes] = mm(mixed, cot, 0, 0)
            return carry

        lax.fori_loop(0, MODEL // COLS, one, 0)

    weight_part(1 - c)
    weight_copy = remote(gwp.at[1 - c], gwr, g_ss.at[0], g_rs.at[0], (twin, me))
    weight_copy.start()
    weight_part(c)

    for step in range(1, SEQ):
        source = (me + step) % SEQ
        arrival(d_recv.at[source], d_ss.at[source], d_rs.at[source])

    def block_copy(step):
        to = (me + step) % SEQ
        return remote(gws.at[to], gwb.at[me], b_ss.at[to], b_rs.at[me], (dp, to))

    def backward_head(head, raw_all):
        queries, keys = q_ref[:, head_lanes(head)], k_ref[:, head_lanes(head)]
        raw = pick_column(raw_all, head)
        b_col = 2.0 * jax.nn.sigmoid(raw)
        r_col, r_row = row_scale(keys), rrow_s[head]
        state, later = head_state(s_recv, head), head_state(d_recv, head)
        grad = gm_s[head]
        delta = insert_s[head] - mm2((erase_s[0, head], erase_s[1, head]), state, 1, 1)
        solved = y_s[head] + mm2((kback_s[0, head], kback_s[1, head]), later, 1, 1)
        scaled = b_col * solved
        gv_ref[:, head_lanes(head)] = scaled.astype(bf16)
        raw_grad = jnp.sum(solved * delta, axis=1, keepdims=True) * jax.nn.sigmoid(-raw)
        delta_parts, scaled_parts = split(delta), split(-scaled)
        score_grad = mm(grad, delta_parts[0], 1, 1) + mm(grad, delta_parts[1], 1, 1)
        frame, step = iota(score_grad.shape, 0), iota(score_grad.shape, 1)
        score_grad = jnp.where(step <= 2 * frame + 1, score_grad, 0.0)
        inner_grad = mm3(scaled_parts, delta_parts, 1, 1)
        row, column = iota(inner_grad.shape, 0), iota(inner_grad.shape, 1)
        inner_grad = jnp.where(column < row, inner_grad, 0.0)
        query_grad = mm(grad, state) + mm((score_grad * r_row).astype(bf16), keys)
        gq_ref[:, head_lanes(head)] = query_grad.astype(bf16)
        key_grad = mm(scaled_parts[0], state) + mm(delta_parts[0], later)
        key_grad = key_grad + mm(score_grad.astype(bf16), queries, 0, 0)
        key_grad = key_grad + mm((inner_grad * r_row).astype(bf16), keys)
        key_grad = key_grad + mm((inner_grad * r_col).astype(bf16), keys, 0, 0)
        unit = keys.astype(f32) * r_col
        along = jnp.sum(key_grad * unit, axis=1, keepdims=True)
        gk_ref[:, head_lanes(head)] = (r_col * (key_grad - unit * along)).astype(bf16)
        return raw_grad

    lane = iota((STEPS, HEADS), 1)

    def backward_pair(index, total):
        raw_all = bcol_ref[...]
        for inner in range(2):
            head = 2 * index + inner
            total = total + jnp.where(lane == head, backward_head(head, raw_all), 0.0)

        @pl.when(index == 0)
        def _():
            arrival(gwr, g_ss.at[0], g_rs.at[0])

            def one(block, carry):
                rows = pl.ds(pl.multiple_of(block * 8, 8), 8)
                gws[block] = gwp[c, rows] + gwr[rows]
                return carry

            lax.fori_loop(0, SEQ, one, 0)
            for step in range(1, SEQ):
                block_copy(step).start()
            gwb[me] = gws[me]

        return total

    gb_ref[...] = lax.fori_loop(0, HEADS // 2, backward_pair, jnp.zeros((STEPS, HEADS), f32))

    for step in range(1, SEQ):
        source = (me + step) % SEQ
        arrival(gwb.at[source], b_ss.at[source], b_rs.at[source])
    total = gwb[0]
    for block in range(1, SEQ):
        total = total + gwb[block]
    gw_ref[...] = total

    for phase in range(6):
        w_sent(phase)
    for step in range(1, SIDE):
        cot_copy(step).wait_send()
        mixed_copy(step).wait_send()
    weight_copy.wait_send()
    for step in range(1, SEQ):
        other = (me + step) % SEQ
        block_copy(step).wait_send()
        remote(t_send.at[other // 2], t_recv.at[me], t_ss.at[other], t_rs.at[me], (dp, other)).wait_send()
        half_rows = pl.ds(pl.multiple_of((other % 2) * HALF, HALF), HALF)
        remote(
            o_send.at[other // 2, half_rows], o_recv.at[me], o_ss.at[other], o_rs.at[me], (dp, other)
        ).wait_send()
        remote(
            z_send.at[other // 2, half_rows], z_recv.at[me], z_ss.at[other], z_rs.at[me], (dp, other)
        ).wait_send()
        remote(s_send.at[other], s_recv.at[me], s_ss.at[other], s_rs.at[me], (dp, other)).wait_send()
        remote(d_send.at[other], d_recv.at[me], d_ss.at[other], d_rs.at[me], (dp, other)).wait_send()


def per_device(queries, key_vectors, values, beta_raw, cotangent, w_out):
    raw_col = beta_raw.reshape(STEPS, HEADS)
    raw_row = jnp.transpose(raw_col).reshape(HEADS, 1, STEPS)
    w_rows = w_out.reshape(8, 2, MODEL // 2).transpose(1, 0, 2).reshape(16, MODEL // 2)
    vmem = pl.BlockSpec(memory_space=pltpu.VMEM)
    dma = pltpu.SemaphoreType.DMA
    out = pl.pallas_call(
        kernel,
        out_shape=(
            jax.ShapeDtypeStruct((FRAMES, MODEL), bf16),
            jax.ShapeDtypeStruct((FRAMES, FEATURES), bf16),
            jax.ShapeDtypeStruct((STEPS, FEATURES), bf16),
            jax.ShapeDtypeStruct((STEPS, FEATURES), bf16),
            jax.ShapeDtypeStruct((STEPS, HEADS), f32),
            jax.ShapeDtypeStruct((8, MODEL), f32),
        ),
        in_specs=[vmem] * 7,
        out_specs=[vmem] * 6,
        scratch_shapes=[
            pltpu.VMEM((SIDE, 2, SIDE, SIDE, 16, MODEL // 2), bf16),
            pltpu.VMEM((FEATURES, MODEL), bf16),
            pltpu.VMEM((SIDE, FRAMES, MODEL), bf16),
            pltpu.VMEM((2, HEADS, STEPS, DIM), bf16),
            pltpu.VMEM((HEADS, STEPS, DIM), f32),
            pltpu.VMEM((2, HEADS, STEPS, DIM), bf16),
            pltpu.VMEM((2, HEADS, STEPS, DIM), bf16),
            pltpu.VMEM((HEADS, FRAMES, DIM), bf16),
            pltpu.VMEM((HEADS, FRAMES, DIM), f32),
            pltpu.VMEM((HEADS, 1, STEPS), f32),
            pltpu.VMEM((HEADS, FRAMES, DIM), bf16),
            pltpu.VMEM((HEADS, STEPS, DIM), f32),
            pltpu.VMEM((HEADS, DIM, DIM), f32),
            pltpu.VMEM((HEADS, DIM, DIM), f32),
            pltpu.VMEM((HEADS, DIM, DIM), bf16),
            pltpu.VMEM((SEQ, DIM, DIM), f32),
            pltpu.VMEM((SEQ, HALF, DIM), f32),
            pltpu.VMEM((SEQ, HALF, DIM), bf16),
            pltpu.VMEM((SEQ, HALF, DIM), bf16),
            pltpu.VMEM((SEQ, HALF, DIM), bf16),
            pltpu.VMEM((SEQ, HALF, DIM), bf16),
            pltpu.VMEM((SEQ, HALF, DIM), bf16),
            pltpu.VMEM((HEADS, FRAMES, DIM), bf16),
            pltpu.VMEM((FRAMES, FEATURES), bf16),
            pltpu.VMEM((2, SIDE, FRAMES, DIM), bf16),
            pltpu.VMEM((2, DIM, MODEL), f32),
            pltpu.VMEM((DIM, MODEL), f32),
            pltpu.VMEM((SEQ, 8, MODEL), f32),
            pltpu.VMEM((SEQ, 8, MODEL), f32),
            dma((18,)), dma((18,)), dma((3,)), dma((3,)),
            dma((SEQ,)), dma((SEQ,)), dma((SEQ,)), dma((SEQ,)), dma((SEQ,)), dma((SEQ,)),
            dma((SEQ,)), dma((SEQ,)), dma((SEQ,)), dma((SEQ,)),
            dma((3,)), dma((3,)), dma((1,)), dma((1,)), dma((SEQ,)), dma((SEQ,)),
        ],
        compiler_params=pltpu.CompilerParams(
            collective_id=0, has_side_effects=True, vmem_limit_bytes=60 * 1024 * 1024
        ),
        name="delta_product",
    )(
        queries[0],
        key_vectors[0].reshape(STEPS, FEATURES),
        values[0].reshape(STEPS, FEATURES),
        raw_col,
        raw_row,
        cotangent[0],
        w_rows,
    )
    projected, grad_query, grad_key, grad_value, grad_raw, grad_weight = out
    return (
        projected[None],
        grad_query[None],
        grad_key.reshape(1, FRAMES, 2, FEATURES),
        grad_value.reshape(1, FRAMES, 2, FEATURES),
        grad_raw.reshape(1, FRAMES, 2 * HEADS),
        grad_weight,
    )


def solution(mesh):
    in_specs = (
        P("dp", "seq", None),
        P("dp", "seq", None, None),
        P("dp", "seq", None, None),
        P("dp", "seq", None),
        P("dp", "seq", None),
        P(("dp", "seq"), None),
    )
    out_specs = (
        P("dp", "seq", None),
        P("dp", "seq", None),
        P("dp", "seq", None, None),
        P("dp", "seq", None, None),
        P("dp", "seq", None),
        P(("dp", "seq"), None),
    )
    return jax.shard_map(
        per_device, mesh=mesh, in_specs=in_specs, out_specs=out_specs, check_vma=False
    )
```

time: 1150 us -> 113 us (0.10)
  the two profiles are of different devices: /device:TPU:0 before, /device:TPU:48 now
where the time goes in v1:
time: 113 us
  Pallas kernels  100 us (88%)
  local copies, waits for them, and re-layouts  12 us (11%)
    pallas_call x1, Pallas kernels, per_device(): pl.pallas_call(kernel, out_shape=(jax.ShapeDtypeStruct((FRAMES, MODEL), b...  100 us
    unnamed x17, local copies, waits for them, and re-layouts  4.11 us

profile of v1, /device:TPU:48, one launch (start us, length us, event | category | flops | bytes accessed | tf_op | source)
XLA Modules:
  0.0 112.7 jit_solution(11854426436262591500)
XLA Ops:
  0.6 0.8 copy.14
  1.4 0.1 reshape.33.bcol_ref
  1.5 0.0 copy-start
  1.5 0.1 copy.15
  1.6 0.6 reshape.34.brow_ref
  2.2 0.0 copy-start.1
  2.2 2.1 %reshape_squeeze.6.k_ref = bf16[256,1024]{1,0:T(8,128)(2,1)} reshape(bf16[1,128,2,1024]{3,2,1,0:T(2,128)(2,1)} %param.7) | data formatting | bytes 1048576 | tf_op jit(solution)/shard_map/reshape;squeeze | solution.py:573
  4.3 0.0 copy-done
  4.3 0.0 copy-done.1
  4.3 1.0 reshape_squeeze.7.v_ref
  5.3 100.0 %delta_product.1 = (bf16[128,2048]{1,0:T(8,128)(2,1)}, bf16[128,1024]{1,0:T(8,128)(2,1)}, bf16[256,1024]{1,0:T(8,128)(2,1)}, bf16[256,1024]{1,0:T(8,128)(2,1)}, f32[256,8]{1,0:T(8,128)}, /*index=5*/f32[8,2048]{1,0:T(8,128)}) custom-call(bf16[128,1024]{1,0:T(8,128)(2,1)} %bitcast.12, bf16[256,1024]{1,0:T(8,128)(2,1)} %reshape_squeeze.6.k_ref, ...), custom_call_target="tpu_custom_call" | custom-call | tf_op jit(solution)/shard_map/delta_product/pallas_call | solution.py:520
  105.3 1.0 reshape.39
  106.3 0.7 copy.16
  107.0 0.0 copy-start.3
  107.0 2.1 %reshape.37 = bf16[1,128,2,1024]{3,2,1,0:T(2,128)(2,1)} reshape(bf16[256,1024]{1,0:T(8,128)(2,1)} %get-tuple-element.14) | data formatting | bytes 1048576 | tf_op jit(solution)/shard_map/reshape | solution.py:584
  109.1 0.0 copy-done.3
  109.1 0.0 copy-start.2
  109.1 1.0 reshape.38
  110.1 0.0 copy-done.2
  110.1 0.0 copy-start.4
  110.1 0.8 copy.20
  110.9 0.3 copy-done.4
  111.2 0.0 copy-start.5
  111.2 0.7 copy.21
  111.9 0.2 copy-done.5
  112.1 0.6 copy.22
Async XLA Ops:
  1.5 2.8 %copy-start = (f32[256,8]{1,0:T(8,128)}, f32[256,8]{1,0:T(8,128)S(1)}, u32[]{:S(2)}) copy-start(f32[256,8]{1,0:T(8,128)S(1)} %reshape.33.bcol_ref) | copy-start | bytes 24580
  2.2 2.1 %copy-start.1 = (bf16[1,128,2,1024]{3,2,1,0:T(2,128)(2,1)S(1)}, bf16[1,128,2,1024]{3,2,1,0:T(2,128)(2,1)}, u32[]{:S(2)}) copy-start(bf16[1,128,2,1024]{3,2,1,0:T(2,128)(2,1)} %param.8) | copy-start | bytes 1572868
  107.0 2.1 %copy-start.3 = (bf16[256,1024]{1,0:T(8,128)(2,1)S(1)}, bf16[256,1024]{1,0:T(8,128)(2,1)}, u32[]{:S(2)}) copy-start(bf16[256,1024]{1,0:T(8,128)(2,1)} %get-tuple-element.15) | copy-start | bytes 1572868
  109.1 1.0 copy-start.2
  110.1 1.1 copy-start.4
  111.2 0.9 copy-start.5

commit v2 on v1

--- a/solution.py
+++ b/solution.py
@@ -18,6 +18,8 @@
 SEQ = 16
 SIDE = 4
 COLS = 512
+W_AT = 1
+RELAY_AT = 3
 
 
 def mm(a, b, ca=1, cb=0):
@@ -35,6 +37,13 @@
 
 def mm3(a, b, ca=1, cb=0):
     return mm(a[0], b[0], ca, cb) + (mm(a[0], b[1], ca, cb) + mm(a[1], b[0], ca, cb))
+
+
+def thirds(x):
+    high = x.astype(bf16)
+    rest = x - high.astype(f32)
+    middle = rest.astype(bf16)
+    return high, middle, (rest - middle.astype(f32)).astype(bf16)
 
 
 def iota(shape, axis):
@@ -115,13 +124,14 @@
 
 
 def kernel(
-    q_ref, k_ref, v_ref, bcol_ref, brow_ref, cot_ref, w_ref,
+    q_ref, k_ref, v_ref, raw_ref, cot_ref, w_ref,
     proj_ref, gq_ref, gk_ref, gv_ref, gb_ref, gw_ref,
+    bcol_ref, brow_ref,
     wg, wf, cotg, erase_s, insert_s, kback_s, sback_s, reads_s, mixed_s, rrow_s, gm_s, y_s,
     t_send, o_send, z_send, t_recv, o_recv, z_recv,
-    s_send, d_send, s_recv, d_recv, mb_send, mb_full, mb_recv, gwp, gwr, gws, gwb,
-    w_ss, w_rs, c_ss, c_rs, t_ss, t_rs, o_ss, o_rs, z_ss, z_rs, s_ss, s_rs, d_ss, d_rs,
-    m_ss, m_rs, g_ss, g_rs, b_ss, b_rs,
+    s_send, d_send, s_recv, d_recv, mb_send, mb_full, mb_recv, gwp, gwh, gwr, gws, gwb,
+    w_ss, w_rs, wx_ss, wx_rs, e_ss, e_rs, c_ss, c_rs, t_ss, t_rs, o_ss, o_rs, z_ss, z_rs,
+    s_ss, s_rs, d_ss, d_rs, m_ss, m_rs, g_ss, g_rs, b_ss, b_rs,
 ):
     dp, me = lax.axis_index("dp"), lax.axis_index("seq")
     x, c = dp // 2, dp % 2
@@ -131,18 +141,28 @@
     def x_peer(step):
         return ((x + step) % SIDE) * 2 + c, me
 
-    def y_peer(step):
-        return dp, ((y + step) % SIDE) * SIDE + z
-
-    def z_peer(step):
-        return dp, y * SIDE + (z + step) % SIDE
-
     barrier = pltpu.get_barrier_semaphore()
     for step in range(1, SEQ):
         pl.semaphore_signal(barrier, inc=1, device_id=(dp, (me + step) % SEQ), device_id_type=MESH)
     for step in range(1, SIDE):
         pl.semaphore_signal(barrier, inc=1, device_id=x_peer(step), device_id_type=MESH)
     pl.semaphore_signal(barrier, inc=1, device_id=(twin, me), device_id_type=MESH)
+
+    expand = (iota((STEPS, FRAMES), 0) // 2 == iota((STEPS, FRAMES), 1)).astype(bf16)
+    raw_parts = thirds(raw_ref[...])
+    columns = sum(mm(expand, part) for part in raw_parts)
+    bcol_ref[...] = jnp.where(
+        iota((STEPS, HEADS), 0) % 2 == 0, columns[:, :HEADS], columns[:, HEADS:]
+    )
+    rows = sum(mm(part, expand, 0, 1) for part in raw_parts)
+    rows = jnp.where(iota((HEADS, STEPS), 1) % 2 == 0, rows[:HEADS], rows[HEADS:])
+    for head in range(HEADS):
+        brow_ref[head] = rows[head : head + 1]
+    w_wide = w_ref[...].astype(f32)
+    w_halves = jnp.concatenate([w_wide[:, : MODEL // 2], w_wide[:, MODEL // 2 :]], axis=0)
+    wg[x, c, me] = w_halves.astype(bf16)
+    cotg[x] = cot_ref[...]
+
     pl.semaphore_wait(barrier, SEQ - 1 + SIDE - 1 + 1)
 
     def remote(source, target, send_sem, recv_sem, device):
@@ -154,52 +174,59 @@
     def arrival(target, send_sem, recv_sem):
         remote(target, target, send_sem, recv_sem, (twin, me)).wait_recv()
 
-    left, right = pl.ds(0, COLS), pl.ds(COLS, COLS)
-
-    def w_copy(phase, step):
-        if phase == 0:
-            return wg.at[x, c, y, z], wg.at[(x - step + SIDE) % SIDE, c, y, z], x_peer(step)
-        if phase == 1:
-            return wg.at[:, c, y, z, :, left], wg.at[:, c, (y - step + SIDE) % SIDE, z, :, left], y_peer(step)
-        if phase == 2:
-            return wg.at[:, c, y, z, :, right], wg.at[:, c, y, (z - step + SIDE) % SIDE, :, right], z_peer(step)
-        if phase == 3:
-            return wg.at[:, c, :, z, :, left], wg.at[:, c, :, (z - step + SIDE) % SIDE, :, left], z_peer(step)
-        if phase == 4:
-            return wg.at[:, c, y, :, :, right], wg.at[:, c, (y - step + SIDE) % SIDE, :, :, right], y_peer(step)
-        part = left if step == 1 else right
-        return wg.at[:, c, :, :, :, part], wg.at[:, 1 - c, :, :, :, part], (twin, me)
-
-    def w_steps(phase):
-        return range(1, 3) if phase == 5 else range(1, SIDE)
-
-    def w_start(phase):
-        for step in w_steps(phase):
-            source, _, device = w_copy(phase, step)
-            sem = 3 * phase + step - 1
-            remote(source, source, w_ss.at[sem], w_rs.at[sem], device).start()
-
-    def w_arrive(phase):
-        for step in w_steps(phase):
-            _, target, _ = w_copy(phase, step)
-            sem = 3 * phase + step - 1
-            arrival(target, w_ss.at[sem], w_rs.at[sem])
-
-    def w_sent(phase):
-        for step in w_steps(phase):
-            source, _, device = w_copy(phase, step)
-            sem = 3 * phase + step - 1
-            remote(source, source, w_ss.at[sem], w_rs.at[sem], device).wait_send()
-
-    wg[x, c, y, z] = w_ref[...]
-    w_start(0)
-
-    def cot_copy(step):
-        return remote(cot_ref, cotg.at[x], c_ss.at[step - 1], c_rs.at[step - 1], x_peer(step))
-
-    for step in range(1, SIDE):
-        cot_copy(step).start()
-    cotg[x] = cot_ref[...]
+    def w_copy(to):
+        return remote(wg.at[x, c, me], wg.at[x, c, me], w_ss.at[to], w_rs.at[me], (dp, to))
+
+    for step in range(1, SEQ):
+        w_copy((me + step) % SEQ).start()
+
+    before, after, across = (x + 3) % SIDE, (x + 1) % SIDE, (x + 2) % SIDE
+
+    class Ring:
+        def __init__(self, block, send_sems, recv_sems):
+            self.block, self.send_sems, self.recv_sems = block, send_sems, recv_sems
+
+        def copy(self, place, half, sem):
+            ref = self.block(place, half)
+            device = x_peer(1) if sem < 3 else x_peer(3)
+            return remote(ref, ref, self.send_sems.at[sem], self.recv_sems.at[sem], device)
+
+        def arrive(self, place, half, sem):
+            arrival(self.block(place, half), self.send_sems.at[sem], self.recv_sems.at[sem])
+
+        def start(self):
+            for half in range(2):
+                self.copy(x, half, half).start()
+                self.copy(x, 1 - half, 3 + 1 - half).start()
+
+        def relay(self):
+            self.arrive(before, 0, 0)
+            self.copy(before, 0, 2).start()
+            self.arrive(after, 1, 4)
+            self.copy(after, 1, 5).start()
+
+        def near(self):
+            self.arrive(before, 1, 1)
+            self.arrive(after, 0, 3)
+
+        def far(self):
+            self.arrive(across, 0, 2)
+            self.arrive(across, 1, 5)
+
+        def sent(self):
+            for half in range(2):
+                self.copy(x, half, half).wait_send()
+                self.copy(x, half, 3 + half).wait_send()
+            self.copy(before, 0, 2).wait_send()
+            self.copy(after, 1, 5).wait_send()
+
+    w_ring = Ring(lambda place, half: wg.at[place, c, pl.ds(8 * half, 8)], wx_ss, wx_rs)
+    cot_ring = Ring(lambda place, half: cotg.at[place, pl.ds(HALF * half, HALF)], c_ss, c_rs)
+    places = (x, before, after, across)
+
+    def core_copy(index):
+        ref = wg.at[places[index], c]
+        return remote(ref, ref, e_ss.at[index], e_rs.at[index], (twin, me))
 
     def head_lanes(head):
         return pl.ds(pl.multiple_of(head * DIM, DIM), DIM)
@@ -234,6 +261,7 @@
         for inner, result in enumerate(local_forward(heads)):
             head = 2 * pair + inner
             erase, insert, key_back, score_back, transit, offset, reads, mixed, r_row = result
+            offset = offset.astype(bf16)
             t_send[head] = transit
             o_send[head] = offset
             for half in range(2):
@@ -257,25 +285,25 @@
             mixed_s[head] = mixed
             rrow_s[head] = r_row
 
-        @pl.when(index == 0)
+        @pl.when(index == W_AT)
         def _():
-            w_arrive(0)
-            w_start(1)
-            w_start(2)
-
-        @pl.when(index == 1)
+            for step in range(1, SEQ):
+                source = (me + step) % SEQ
+                arrival(wg.at[x, c, source], w_ss.at[source], w_rs.at[source])
+            w_ring.start()
+            core_copy(0).start()
+
+        @pl.when(index == RELAY_AT)
         def _():
-            w_arrive(1)
-            w_start(3)
-            w_arrive(2)
-            w_start(4)
+            w_ring.relay()
+            w_ring.near()
+            core_copy(1).start()
+            core_copy(2).start()
 
         return carry
 
     lax.fori_loop(0, HEADS // 2, forward_pair, 0)
-    w_arrive(3)
-    w_arrive(4)
-    w_start(5)
+    cot_ring.start()
 
     for step in range(1, SEQ):
         source = (me + step) % SEQ
@@ -297,29 +325,32 @@
 
     def carry_state(segment, state):
         send_state(s_send, s_recv, state, segment, s_ss, s_rs)
-        return mm3(split(state), split(t_recv[segment]), 1, 1) + o_recv[segment]
+        return mm3(split(state), split(t_recv[segment]), 1, 1) + o_recv[segment].astype(f32)
 
     last_state = lax.fori_loop(0, SEQ - 1, carry_state, jnp.zeros((HALF, DIM), f32))
     send_state(s_send, s_recv, last_state, SEQ - 1, s_ss, s_rs)
 
-    def order_rows(core):
+    w_ring.far()
+    core_copy(3).start()
+
+    def order_rows(place, core):
         def one(index, carry):
-            across, block = index // 8, index % 8
-            row, column = block // 2, 2 * (block % 2)
-            first = wg[across, core, row, column].astype(f32)
-            second = wg[across, core, row, column + 1].astype(f32)
-            start = pl.multiple_of(((across * 2 + core) * 8 + block) * 16, 16)
+            first = wg[place, core, 2 * index].astype(f32)
+            second = wg[place, core, 2 * index + 1].astype(f32)
+            start = pl.multiple_of(((place * 2 + core) * 8 + index) * 16, 16)
             top = jnp.concatenate([first[:8], second[:8]], axis=0)
             bottom = jnp.concatenate([first[8:], second[8:]], axis=0)
             wf[pl.ds(start, 16), pl.ds(0, MODEL // 2)] = top.astype(bf16)
             wf[pl.ds(start, 16), pl.ds(MODEL // 2, MODEL // 2)] = bottom.astype(bf16)
             return carry
 
-        lax.fori_loop(0, 32, one, 0)
-
-    order_rows(c)
-    w_arrive(5)
-    order_rows(1 - c)
+        lax.fori_loop(0, 8, one, 0, unroll=2)
+
+    for place in places:
+        order_rows(place, c)
+    for index, place in enumerate(places):
+        arrival(wg.at[place, 1 - c], e_ss.at[index], e_rs.at[index])
+        order_rows(place, 1 - c)
 
     def gradient_pair(index, carry):
         pair = (index + y) % SIDE
@@ -345,6 +376,7 @@
         return carry
 
     lax.fori_loop(0, HEADS // 2, gradient_pair, 0)
+    cot_ring.relay()
 
     def early_gradient(head, carry):
         y_s[head] = mm2((sback_s[0, head], sback_s[1, head]), gm_s[head])
@@ -397,26 +429,30 @@
 
     lax.fori_loop(0, MODEL // COLS, project, 0)
 
+    cot_ring.near()
+    cot_ring.far()
     for step in range(1, SIDE):
         source = (x - step + SIDE) % SIDE
-        arrival(cotg.at[source], c_ss.at[step - 1], c_rs.at[step - 1])
         arrival(mb_recv.at[:, source], m_ss.at[step - 1], m_rs.at[step - 1])
 
-    def weight_part(inner):
+    def weight_chunk(inner, chunk):
         mixed = mb_recv[inner].reshape(SIDE * FRAMES, DIM)
-
-        def one(index, carry):
-            lanes = pl.ds(pl.multiple_of(index * COLS, COLS), COLS)
-            cot = cotg[:, :, lanes].reshape(SIDE * FRAMES, COLS)
-            gwp[inner, :, lanes] = mm(mixed, cot, 0, 0)
-            return carry
-
-        lax.fori_loop(0, MODEL // COLS, one, 0)
-
-    weight_part(1 - c)
-    weight_copy = remote(gwp.at[1 - c], gwr, g_ss.at[0], g_rs.at[0], (twin, me))
-    weight_copy.start()
-    weight_part(c)
+        lanes = pl.ds(chunk * COLS, COLS)
+        return lanes, mm(mixed, cotg[:, :, lanes].reshape(SIDE * FRAMES, COLS), 0, 0)
+
+    def weight_copy(chunk):
+        lanes = pl.ds(chunk * COLS, COLS)
+        return remote(
+            gwh.at[:, lanes], gwr.at[:, lanes], g_ss.at[chunk], g_rs.at[chunk], (twin, me)
+        )
+
+    for chunk in range(MODEL // COLS):
+        lanes, part = weight_chunk(1 - c, chunk)
+        gwh[:, lanes] = part.astype(bf16)
+        weight_copy(chunk).start()
+    for chunk in range(MODEL // COLS):
+        lanes, part = weight_chunk(c, chunk)
+        gwp[:, lanes] = part
 
     for step in range(1, SEQ):
         source = (me + step) % SEQ
@@ -466,39 +502,53 @@
 
         @pl.when(index == 0)
         def _():
-            arrival(gwr, g_ss.at[0], g_rs.at[0])
-
-            def one(block, carry):
-                rows = pl.ds(pl.multiple_of(block * 8, 8), 8)
-                gws[block] = gwp[c, rows] + gwr[rows]
+            for chunk in range(MODEL // COLS):
+                lanes = pl.ds(chunk * COLS, COLS)
+                arrival(gwr.at[:, lanes], g_ss.at[chunk], g_rs.at[chunk])
+
+            def one(index, carry):
+                rows = pl.ds(pl.multiple_of(index * 16, 16), 16)
+                block = gwp[rows] + gwr[rows].astype(f32)
+                for inner in range(2):
+                    part = block[8 * inner : 8 * inner + 8]
+                    halves = [part[:, : MODEL // 2], part[:, MODEL // 2 :]]
+                    gws[2 * index + inner] = jnp.concatenate(halves, axis=0).astype(bf16)
                 return carry
 
-            lax.fori_loop(0, SEQ, one, 0)
+            lax.fori_loop(0, SEQ // 2, one, 0)
             for step in range(1, SEQ):
                 block_copy(step).start()
             gwb[me] = gws[me]
 
         return total
 
-    gb_ref[...] = lax.fori_loop(0, HEADS // 2, backward_pair, jnp.zeros((STEPS, HEADS), f32))
+    raw_grad = lax.fori_loop(0, HEADS // 2, backward_pair, jnp.zeros((STEPS, HEADS), f32))
+    raw_parts = thirds(raw_grad)
+    for inner in range(2):
+        chosen = 2 * iota((FRAMES, STEPS), 0) + inner == iota((FRAMES, STEPS), 1)
+        chosen = chosen.astype(bf16)
+        gb_ref[:, inner * HEADS : (inner + 1) * HEADS] = sum(mm(chosen, part) for part in raw_parts)
 
     for step in range(1, SEQ):
         source = (me + step) % SEQ
         arrival(gwb.at[source], b_ss.at[source], b_rs.at[source])
-    total = gwb[0]
+    total = gwb[0].astype(f32)
     for block in range(1, SEQ):
-        total = total + gwb[block]
-    gw_ref[...] = total
-
-    for phase in range(6):
-        w_sent(phase)
+        total = total + gwb[block].astype(f32)
+    gw_ref[:, : MODEL // 2] = total[:8]
+    gw_ref[:, MODEL // 2 :] = total[8:]
+
+    w_ring.sent()
+    cot_ring.sent()
+    for index in range(4):
+        core_copy(index).wait_send()
+        weight_copy(index).wait_send()
     for step in range(1, SIDE):
-        cot_copy(step).wait_send()
         mixed_copy(step).wait_send()
-    weight_copy.wait_send()
     for step in range(1, SEQ):
         other = (me + step) % SEQ
         block_copy(step).wait_send()
+        w_copy(other).wait_send()
         remote(t_send.at[other // 2], t_recv.at[me], t_ss.at[other], t_rs.at[me], (dp, other)).wait_send()
         half_rows = pl.ds(pl.multiple_of((other % 2) * HALF, HALF), HALF)
         remote(
@@ -512,9 +562,6 @@
 
 
 def per_device(queries, key_vectors, values, beta_raw, cotangent, w_out):
-    raw_col = beta_raw.reshape(STEPS, HEADS)
-    raw_row = jnp.transpose(raw_col).reshape(HEADS, 1, STEPS)
-    w_rows = w_out.reshape(8, 2, MODEL // 2).transpose(1, 0, 2).reshape(16, MODEL // 2)
     vmem = pl.BlockSpec(memory_space=pltpu.VMEM)
     dma = pltpu.SemaphoreType.DMA
     out = pl.pallas_call(
@@ -524,13 +571,15 @@
             jax.ShapeDtypeStruct((FRAMES, FEATURES), bf16),
             jax.ShapeDtypeStruct((STEPS, FEATURES), bf16),
             jax.ShapeDtypeStruct((STEPS, FEATURES), bf16),
-            jax.ShapeDtypeStruct((STEPS, HEADS), f32),
+            jax.ShapeDtypeStruct((FRAMES, 2 * HEADS), f32),
             jax.ShapeDtypeStruct((8, MODEL), f32),
         ),
-        in_specs=[vmem] * 7,
+        in_specs=[vmem] * 6,
         out_specs=[vmem] * 6,
         scratch_shapes=[
-            pltpu.VMEM((SIDE, 2, SIDE, SIDE, 16, MODEL // 2), bf16),
+            pltpu.VMEM((STEPS, HEADS), f32),
+            pltpu.VMEM((HEADS, 1, STEPS), f32),
+            pltpu.VMEM((SIDE, 2, SEQ, 16, MODEL // 2), bf16),
             pltpu.VMEM((FEATURES, MODEL), bf16),
             pltpu.VMEM((SIDE, FRAMES, MODEL), bf16),
             pltpu.VMEM((2, HEADS, STEPS, DIM), bf16),
@@ -543,10 +592,10 @@
             pltpu.VMEM((HEADS, FRAMES, DIM), bf16),
             pltpu.VMEM((HEADS, STEPS, DIM), f32),
             pltpu.VMEM((HEADS, DIM, DIM), f32),
-            pltpu.VMEM((HEADS, DIM, DIM), f32),
+            pltpu.VMEM((HEADS, DIM, DIM), bf16),
             pltpu.VMEM((HEADS, DIM, DIM), bf16),
             pltpu.VMEM((SEQ, DIM, DIM), f32),
-            pltpu.VMEM((SEQ, HALF, DIM), f32),
+            pltpu.VMEM((SEQ, HALF, DIM), bf16),
             pltpu.VMEM((SEQ, HALF, DIM), bf16),
             pltpu.VMEM((SEQ, HALF, DIM), bf16),
             pltpu.VMEM((SEQ, HALF, DIM), bf16),
@@ -555,14 +604,15 @@
             pltpu.VMEM((HEADS, FRAMES, DIM), bf16),
             pltpu.VMEM((FRAMES, FEATURES), bf16),
             pltpu.VMEM((2, SIDE, FRAMES, DIM), bf16),
-            pltpu.VMEM((2, DIM, MODEL), f32),
             pltpu.VMEM((DIM, MODEL), f32),
-            pltpu.VMEM((SEQ, 8, MODEL), f32),
-            pltpu.VMEM((SEQ, 8, MODEL), f32),
-            dma((18,)), dma((18,)), dma((3,)), dma((3,)),
+            pltpu.VMEM((DIM, MODEL), bf16),
+            pltpu.VMEM((DIM, MODEL), bf16),
+            pltpu.VMEM((SEQ, 16, MODEL // 2), bf16),
+            pltpu.VMEM((SEQ, 16, MODEL // 2), bf16),
+            dma((SEQ,)), dma((SEQ,)), dma((6,)), dma((6,)), dma((4,)), dma((4,)), dma((6,)), dma((6,)),
             dma((SEQ,)), dma((SEQ,)), dma((SEQ,)), dma((SEQ,)), dma((SEQ,)), dma((SEQ,)),
             dma((SEQ,)), dma((SEQ,)), dma((SEQ,)), dma((SEQ,)),
-            dma((3,)), dma((3,)), dma((1,)), dma((1,)), dma((SEQ,)), dma((SEQ,)),
+            dma((3,)), dma((3,)), dma((4,)), dma((4,)), dma((SEQ,)), dma((SEQ,)),
         ],
         compiler_params=pltpu.CompilerParams(
             collective_id=0, has_side_effects=True, vmem_limit_bytes=60 * 1024 * 1024
@@ -572,10 +622,9 @@
         queries[0],
         key_vectors[0].reshape(STEPS, FEATURES),
         values[0].reshape(STEPS, FEATURES),
-        raw_col,
-        raw_row,
+        beta_raw[0],
         cotangent[0],
-        w_rows,
+        w_out,
     )
     projected, grad_query, grad_key, grad_value, grad_raw, grad_weight = out
     return (
@@ -583,7 +632,7 @@
         grad_query[None],
         grad_key.reshape(1, FRAMES, 2, FEATURES),
         grad_value.reshape(1, FRAMES, 2, FEATURES),
-        grad_raw.reshape(1, FRAMES, 2 * HEADS),
+        grad_raw[None],
         grad_weight,
     )
 

time: 113 us -> 90.2 us (0.80)
  the two profiles are of different devices: /device:TPU:48 before, /device:TPU:0 now
where the time goes in v2:
time: 90.2 us; the launch traced here: 89.8 us
  Pallas kernels  77.4 us (86%)
  local copies, waits for them, and re-layouts  11.7 us (13%)
    pallas_call x1, Pallas kernels, per_device(): pl.pallas_call(kernel, out_shape=(jax.ShapeDtypeStruct((FRAMES, MODEL), b...  77.4 us
    unnamed x15, local copies, waits for them, and re-layouts  5.57 us
    another operation x1, local copies, waits for them, and re-layouts, per_device(): key_vectors[0].reshape(STEPS, FEATURES)  2.09 us
    reshape x1, local copies, waits for them, and re-layouts, per_device(): grad_key.reshape(1, FRAMES, 2, FEATURES)  2.09 us

profile of v2, /device:TPU:0, one launch (start us, length us, event | category | flops | bytes accessed | tf_op | source)
XLA Modules:
  0.0 89.8 jit_solution(17518770674162688651)
XLA Ops:
  0.6 1.4 %copy.12 = f32[1,128,16]{2,1,0:T(8,128)} copy(f32[1,128,16]{1,2,0:T(8,128)} %param.9) | data formatting | bytes 16384 | tf_op args[3]
  2.1 0.0 copy-start
  2.1 2.1 %reshape_squeeze.6.k_ref = bf16[256,1024]{1,0:T(8,128)(2,1)} reshape(bf16[1,128,2,1024]{3,2,1,0:T(2,128)(2,1)} %param.7) | data formatting | bytes 1048576 | tf_op jit(solution)/shard_map/reshape;squeeze | solution.py:623
  4.2 0.0 copy-done
  4.2 1.0 %reshape_squeeze.7.v_ref = bf16[256,1024]{1,0:T(8,128)(2,1)} reshape(bf16[1,128,2,1024]{3,2,1,0:T(2,128)(2,1)S(1)} %copy-done) | data formatting | bytes 1048576 | tf_op jit(solution)/shard_map/reshape;squeeze | solution.py:624
  5.1 77.4 %delta_product.1 = (bf16[128,2048]{1,0:T(8,128)(2,1)}, bf16[128,1024]{1,0:T(8,128)(2,1)}, bf16[256,1024]{1,0:T(8,128)(2,1)}, bf16[256,1024]{1,0:T(8,128)(2,1)}, f32[128,16]{1,0:T(8,128)}, /*index=5*/f32[8,2048]{1,0:T(8,128)}) custom-call(bf16[128,1024]{1,0:T(8,128)(2,1)} %bitcast.9, bf16[256,1024]{1,0:T(8,128)(2,1)} %reshape_squeeze.6.k_ref, ...), custom_call_target="tpu_custom_call" | custom-call | tf_op jit(solution)/shard_map/delta_product/pallas_call | solution.py:567
  82.5 1.5 %copy.13 = f32[1,128,16]{1,2,0:T(8,128)} copy(f32[1,128,16]{2,1,0:T(8,128)} %bitcast.11) | data formatting | bytes 16384
  84.0 0.0 copy-start.2
  84.0 2.1 %reshape.18 = bf16[1,128,2,1024]{3,2,1,0:T(2,128)(2,1)} reshape(bf16[256,1024]{1,0:T(8,128)(2,1)} %get-tuple-element.14) | data formatting | bytes 1048576 | tf_op jit(solution)/shard_map/reshape | solution.py:633
  86.1 0.0 copy-done.2
  86.1 0.0 copy-start.1
  86.1 1.0 %reshape.19 = bf16[1,128,2,1024]{3,2,1,0:T(2,128)(2,1)} reshape(bf16[256,1024]{1,0:T(8,128)(2,1)S(1)} %copy-done.2) | data formatting | bytes 1048576 | tf_op jit(solution)/shard_map/reshape | solution.py:634
  87.1 0.0 copy-done.1
  87.2 0.0 copy-start.3
  87.2 0.8 copy.17
  88.0 0.3 copy-done.3
  88.3 0.0 copy-start.4
  88.3 0.7 copy.18
  89.0 0.2 copy-done.4
  89.1 0.6 copy.19
Async XLA Ops:
  2.1 2.1 %copy-start = (bf16[1,128,2,1024]{3,2,1,0:T(2,128)(2,1)S(1)}, bf16[1,128,2,1024]{3,2,1,0:T(2,128)(2,1)}, u32[]{:S(2)}) copy-start(bf16[1,128,2,1024]{3,2,1,0:T(2,128)(2,1)} %param.8) | copy-start | bytes 1572868
  84.0 2.1 %copy-start.2 = (bf16[256,1024]{1,0:T(8,128)(2,1)S(1)}, bf16[256,1024]{1,0:T(8,128)(2,1)}, u32[]{:S(2)}) copy-start(bf16[256,1024]{1,0:T(8,128)(2,1)} %get-tuple-element.15) | copy-start | bytes 1572868
  86.1 1.0 %copy-start.1 = (bf16[128,2048]{1,0:T(8,128)(2,1)S(1)}, bf16[128,2048]{1,0:T(8,128)(2,1)}, u32[]{:S(2)}) copy-start(bf16[128,2048]{1,0:T(8,128)(2,1)} %get-tuple-element.12) | copy-start | bytes 1572868
  87.2 1.1 %copy-start.3 = (bf16[128,1024]{1,0:T(8,128)(2,1)S(1)}, bf16[128,1024]{1,0:T(8,128)(2,1)}, u32[]{:S(2)}) copy-start(bf16[128,1024]{1,0:T(8,128)(2,1)} %get-tuple-element.13) | copy-start | bytes 786436
  88.3 0.9 copy-start.4

commit v3 on v2

--- a/solution.py
+++ b/solution.py
@@ -19,7 +19,9 @@
 SIDE = 4
 COLS = 512
 W_AT = 1
-RELAY_AT = 3
+RELAY_AT = 5
+WEIGHT_AT = 0
+BLOCK_AT = 1
 
 
 def mm(a, b, ca=1, cb=0):
@@ -76,9 +78,9 @@
     return lax.rsqrt(jnp.sum(wide * wide, axis=1, keepdims=True) + NORM_EPS)
 
 
-def local_forward(heads):
+def local_transits(heads):
     lows, scales = [], []
-    for queries, keys, values, raw_col, raw_row in heads:
+    for keys, values, raw_col, raw_row in heads:
         inner = mm(keys, keys, 1, 1)
         rows, columns = iota(inner.shape, 0), iota(inner.shape, 1)
         squares = jnp.sum(jnp.where(rows == columns, inner, 0.0), axis=0, keepdims=True)
@@ -92,7 +94,7 @@
         blocks += [low[:DIM, :DIM], low[DIM:, DIM:]]
     inverses = unit_lower_inverse(blocks)
     results = []
-    for index, (queries, keys, values, raw_col, raw_row) in enumerate(heads):
+    for index, (keys, values, raw_col, raw_row) in enumerate(heads):
         r_col, r_row, b_col, b_row = scales[index]
         upper, lower = inverses[2 * index], inverses[2 * index + 1]
         corner = mm3(split(lower), split(mm3(split(lows[index][DIM:, :DIM]), split(upper))))
@@ -103,30 +105,36 @@
             ],
             axis=0,
         )
-        written = inverse * b_row
-        erase = mm2(split(written * r_row), keys)
-        insert = mm2(split(written), values)
+        erase = mm2(split(inverse * (b_row * r_row)), keys)
         key_back = mm2(split(inverse * r_col), keys, 0, 0)
-        scores = mm(queries, keys, 1, 1) * r_row
-        frame, step = iota(scores.shape, 0), iota(scores.shape, 1)
-        scores = jnp.where(step <= 2 * frame + 1, scores, 0.0)
-        score_back = mm3(split(inverse), split(scores), 0, 1)
         eye = (iota((DIM, DIM), 0) == iota((DIM, DIM), 1)).astype(f32)
         erase_scaled = split(erase * r_col)
         transit = eye - (mm(keys, erase_scaled[0], 0, 0) + mm(keys, erase_scaled[1], 0, 0))
         back_scaled = split(key_back * b_col)
         offset = mm(values, back_scaled[0], 0, 0) + mm(values, back_scaled[1], 0, 0)
-        weighted = score_back * b_col
-        reads = queries.astype(f32) - mm2(split(weighted * r_col), keys, 0, 0)
-        mixed = mm2(split(weighted), values, 0, 0)
-        results.append((erase, insert, key_back, score_back, transit, offset, reads, mixed, r_row))
+        results.append((inverse, erase, key_back, transit, offset, r_row))
     return results
+
+
+def local_reads(queries, keys, values, raw_col, raw_row, inverse_parts, r_row):
+    r_col = row_scale(keys)
+    b_col, b_row = 2.0 * jax.nn.sigmoid(raw_col), 2.0 * jax.nn.sigmoid(raw_row)
+    inverse = inverse_parts[0].astype(f32) + inverse_parts[1].astype(f32)
+    insert = mm2(split(inverse * b_row), values)
+    scores = mm(queries, keys, 1, 1) * r_row
+    frame, step = iota(scores.shape, 0), iota(scores.shape, 1)
+    scores = jnp.where(step <= 2 * frame + 1, scores, 0.0)
+    score_back = mm3(inverse_parts, split(scores), 0, 1)
+    weighted = score_back * b_col
+    reads = queries.astype(f32) - mm2(split(weighted * r_col), keys, 0, 0)
+    mixed = mm2(split(weighted), values, 0, 0)
+    return insert, score_back, reads, mixed
 
 
 def kernel(
     q_ref, k_ref, v_ref, raw_ref, cot_ref, w_ref,
     proj_ref, gq_ref, gk_ref, gv_ref, gb_ref, gw_ref,
-    bcol_ref, brow_ref,
+    bcol_ref, brow_ref, k_s, v_s, inv_s,
     wg, wf, cotg, erase_s, insert_s, kback_s, sback_s, reads_s, mixed_s, rrow_s, gm_s, y_s,
     t_send, o_send, z_send, t_recv, o_recv, z_recv,
     s_send, d_send, s_recv, d_recv, mb_send, mb_full, mb_recv, gwp, gwh, gwr, gws, gwb,
@@ -150,11 +158,11 @@
 
     expand = (iota((STEPS, FRAMES), 0) // 2 == iota((STEPS, FRAMES), 1)).astype(bf16)
     raw_parts = thirds(raw_ref[...])
-    columns = sum(mm(expand, part) for part in raw_parts)
+    columns = sum(mm(expand, part, 1, 1) for part in raw_parts)
     bcol_ref[...] = jnp.where(
         iota((STEPS, HEADS), 0) % 2 == 0, columns[:, :HEADS], columns[:, HEADS:]
     )
-    rows = sum(mm(part, expand, 0, 1) for part in raw_parts)
+    rows = sum(mm(part, expand, 1, 1) for part in raw_parts)
     rows = jnp.where(iota((HEADS, STEPS), 1) % 2 == 0, rows[:HEADS], rows[HEADS:])
     for head in range(HEADS):
         brow_ref[head] = rows[head : head + 1]
@@ -244,23 +252,18 @@
         rows = pl.ds(half * HALF, HALF)
         return remote(z_send.at[head, rows], z_recv.at[me], z_ss.at[owner], z_rs.at[me], (dp, owner))
 
-    def forward_pair(index, carry):
+    def transit_pair(index, carry):
         pair = (index + y) % SIDE
         heads = []
         for inner in range(2):
             head = 2 * pair + inner
-            heads.append(
-                (
-                    q_ref[:, head_lanes(head)],
-                    k_ref[:, head_lanes(head)],
-                    v_ref[:, head_lanes(head)],
-                    pick_column(bcol_ref[...], head),
-                    brow_ref[head],
-                )
-            )
-        for inner, result in enumerate(local_forward(heads)):
+            keys = k_ref[:, :, head_lanes(head)].reshape(STEPS, DIM)
+            values = v_ref[:, :, head_lanes(head)].reshape(STEPS, DIM)
+            k_s[head], v_s[head] = keys, values
+            heads.append((keys, values, pick_column(bcol_ref[...], head), brow_ref[head]))
+        for inner, result in enumerate(local_transits(heads)):
             head = 2 * pair + inner
-            erase, insert, key_back, score_back, transit, offset, reads, mixed, r_row = result
+            inverse, erase, key_back, transit, offset, r_row = result
             offset = offset.astype(bf16)
             t_send[head] = transit
             o_send[head] = offset
@@ -277,14 +280,29 @@
                     t_recv[me] = transit
                     o_recv[me] = offset[half * HALF : (half + 1) * HALF]
 
+            inv_s[0, head], inv_s[1, head] = split(inverse)
             erase_s[0, head], erase_s[1, head] = split(erase)
+            kback_s[0, head], kback_s[1, head] = split(key_back)
+            rrow_s[head] = r_row
+        advance(index)
+        return carry
+
+    def reads_pair(index, carry):
+        for inner in range(2):
+            head = 2 * index + inner
+            insert, score_back, reads, mixed = local_reads(
+                q_ref[:, head_lanes(head)], k_s[head], v_s[head],
+                pick_column(bcol_ref[...], head), brow_ref[head],
+                (inv_s[0, head], inv_s[1, head]), rrow_s[head],
+            )
             insert_s[head] = insert
-            kback_s[0, head], kback_s[1, head] = split(key_back)
             sback_s[0, head], sback_s[1, head] = split(score_back)
             reads_s[head] = reads.astype(bf16)
             mixed_s[head] = mixed
-            rrow_s[head] = r_row
-
+        advance(index + HEADS // 2)
+        return carry
+
+    def advance(index):
         @pl.when(index == W_AT)
         def _():
             for step in range(1, SEQ):
@@ -300,38 +318,11 @@
             core_copy(1).start()
             core_copy(2).start()
 
-        return carry
-
-    lax.fori_loop(0, HEADS // 2, forward_pair, 0)
-    cot_ring.start()
-
-    for step in range(1, SEQ):
-        source = (me + step) % SEQ
-        arrival(t_recv.at[source], t_ss.at[source], t_rs.at[source])
-        arrival(o_recv.at[source], o_ss.at[source], o_rs.at[source])
-
-    def send_state(buffer, target, value, segment, send_sems, recv_sems):
-        buffer[segment] = value.astype(bf16)
-
-        @pl.when(segment != me)
-        def _():
-            remote(
-                buffer.at[segment], target.at[me], send_sems.at[segment], recv_sems.at[me], (dp, segment)
-            ).start()
-
-        @pl.when(segment == me)
-        def _():
-            target[me] = value.astype(bf16)
-
-    def carry_state(segment, state):
-        send_state(s_send, s_recv, state, segment, s_ss, s_rs)
-        return mm3(split(state), split(t_recv[segment]), 1, 1) + o_recv[segment].astype(f32)
-
-    last_state = lax.fori_loop(0, SEQ - 1, carry_state, jnp.zeros((HALF, DIM), f32))
-    send_state(s_send, s_recv, last_state, SEQ - 1, s_ss, s_rs)
-
+    lax.fori_loop(0, HEADS // 2, transit_pair, 0)
+    lax.fori_loop(0, HEADS // 2, reads_pair, 0)
     w_ring.far()
     core_copy(3).start()
+    cot_ring.start()
 
     def order_rows(place, core):
         def one(index, carry):
@@ -376,13 +367,46 @@
         return carry
 
     lax.fori_loop(0, HEADS // 2, gradient_pair, 0)
-    cot_ring.relay()
 
     def early_gradient(head, carry):
         y_s[head] = mm2((sback_s[0, head], sback_s[1, head]), gm_s[head])
         return carry
 
     lax.fori_loop(0, HEADS, early_gradient, 0)
+
+    for step in range(1, SEQ):
+        source = (me + step) % SEQ
+        arrival(t_recv.at[source], t_ss.at[source], t_rs.at[source])
+        arrival(o_recv.at[source], o_ss.at[source], o_rs.at[source])
+        arrival(z_recv.at[source], z_ss.at[source], z_rs.at[source])
+
+    def send_state(buffer, target, value, segment, send_sems, recv_sems):
+        buffer[segment] = value.astype(bf16)
+
+        @pl.when(segment != me)
+        def _():
+            remote(
+                buffer.at[segment], target.at[me], send_sems.at[segment], recv_sems.at[me], (dp, segment)
+            ).start()
+
+        @pl.when(segment == me)
+        def _():
+            target[me] = value.astype(bf16)
+
+    def carry_both(index, carry):
+        state, adjoint = carry
+        last = SEQ - 1 - index
+        send_state(s_send, s_recv, state, index, s_ss, s_rs)
+        send_state(d_send, d_recv, adjoint, last, d_ss, d_rs)
+        state = mm3(split(state), split(t_recv[index]), 1, 1) + o_recv[index].astype(f32)
+        adjoint = mm3(split(adjoint), split(t_recv[last])) + z_recv[last].astype(f32)
+        return state, adjoint
+
+    empty = jnp.zeros((HALF, DIM), f32)
+    state, adjoint = lax.fori_loop(0, SEQ - 1, carry_both, (empty, empty))
+    send_state(s_send, s_recv, state, SEQ - 1, s_ss, s_rs)
+    send_state(d_send, d_recv, adjoint, 0, d_ss, d_rs)
+    cot_ring.relay()
 
     for step in range(1, SEQ):
         source = (me + step) % SEQ
@@ -410,30 +434,12 @@
     mb_recv[0, x] = mb_send[2 * x]
     mb_recv[1, x] = mb_send[2 * x + 1]
 
-    for step in range(1, SEQ):
-        source = (me + step) % SEQ
-        arrival(z_recv.at[source], z_ss.at[source], z_rs.at[source])
-
-    def carry_adjoint(index, state):
-        segment = SEQ - 1 - index
-        send_state(d_send, d_recv, state, segment, d_ss, d_rs)
-        return mm3(split(state), split(t_recv[segment])) + z_recv[segment].astype(f32)
-
-    first_adjoint = lax.fori_loop(0, SEQ - 1, carry_adjoint, jnp.zeros((HALF, DIM), f32))
-    send_state(d_send, d_recv, first_adjoint, 0, d_ss, d_rs)
-
     def project(index, carry):
         lanes = pl.ds(pl.multiple_of(index * COLS, COLS), COLS)
         proj_ref[:, lanes] = mm(mb_full[...], wf[:, lanes]).astype(bf16)
         return carry
 
     lax.fori_loop(0, MODEL // COLS, project, 0)
-
-    cot_ring.near()
-    cot_ring.far()
-    for step in range(1, SIDE):
-        source = (x - step + SIDE) % SIDE
-        arrival(mb_recv.at[:, source], m_ss.at[step - 1], m_rs.at[step - 1])
 
     def weight_chunk(inner, chunk):
         mixed = mb_recv[inner].reshape(SIDE * FRAMES, DIM)
@@ -446,13 +452,22 @@
             gwh.at[:, lanes], gwr.at[:, lanes], g_ss.at[chunk], g_rs.at[chunk], (twin, me)
         )
 
-    for chunk in range(MODEL // COLS):
-        lanes, part = weight_chunk(1 - c, chunk)
-        gwh[:, lanes] = part.astype(bf16)
-        weight_copy(chunk).start()
-    for chunk in range(MODEL // COLS):
-        lanes, part = weight_chunk(c, chunk)
-        gwp[:, lanes] = part
+    def weight_parts():
+        cot_ring.near()
+        cot_ring.far()
+        for step in range(1, SIDE):
+            source = (x - step + SIDE) % SIDE
+            arrival(mb_recv.at[:, source], m_ss.at[step - 1], m_rs.at[step - 1])
+        for chunk in range(MODEL // COLS):
+            lanes, part = weight_chunk(1 - c, chunk)
+            gwh[:, lanes] = part.astype(bf16)
+            weight_copy(chunk).start()
+        for chunk in range(MODEL // COLS):
+            lanes, part = weight_chunk(c, chunk)
+            gwp[:, lanes] = part
+
+    if WEIGHT_AT < 0:
+        weight_parts()
 
     for step in range(1, SEQ):
         source = (me + step) % SEQ
@@ -463,7 +478,7 @@
         return remote(gws.at[to], gwb.at[me], b_ss.at[to], b_rs.at[me], (dp, to))
 
     def backward_head(head, raw_all):
-        queries, keys = q_ref[:, head_lanes(head)], k_ref[:, head_lanes(head)]
+        queries, keys = q_ref[:, head_lanes(head)], k_s[head]
         raw = pick_column(raw_all, head)
         b_col = 2.0 * jax.nn.sigmoid(raw)
         r_col, r_row = row_scale(keys), rrow_s[head]
@@ -472,7 +487,7 @@
         delta = insert_s[head] - mm2((erase_s[0, head], erase_s[1, head]), state, 1, 1)
         solved = y_s[head] + mm2((kback_s[0, head], kback_s[1, head]), later, 1, 1)
         scaled = b_col * solved
-        gv_ref[:, head_lanes(head)] = scaled.astype(bf16)
+        gv_ref[:, :, head_lanes(head)] = scaled.astype(bf16).reshape(FRAMES, 2, DIM)
         raw_grad = jnp.sum(solved * delta, axis=1, keepdims=True) * jax.nn.sigmoid(-raw)
         delta_parts, scaled_parts = split(delta), split(-scaled)
         score_grad = mm(grad, delta_parts[0], 1, 1) + mm(grad, delta_parts[1], 1, 1)
@@ -489,7 +504,8 @@
         key_grad = key_grad + mm((inner_grad * r_col).astype(bf16), keys, 0, 0)
         unit = keys.astype(f32) * r_col
         along = jnp.sum(key_grad * unit, axis=1, keepdims=True)
-        gk_ref[:, head_lanes(head)] = (r_col * (key_grad - unit * along)).astype(bf16)
+        key_grad = (r_col * (key_grad - unit * along)).astype(bf16)
+        gk_ref[:, :, head_lanes(head)] = key_grad.reshape(FRAMES, 2, DIM)
         return raw_grad
 
     lane = iota((STEPS, HEADS), 1)
@@ -500,7 +516,11 @@
             head = 2 * index + inner
             total = total + jnp.where(lane == head, backward_head(head, raw_all), 0.0)
 
-        @pl.when(index == 0)
+        @pl.when(index == WEIGHT_AT)
+        def _():
+            weight_parts()
+
+        @pl.when(index == BLOCK_AT)
         def _():
             for chunk in range(MODEL // COLS):
                 lanes = pl.ds(chunk * COLS, COLS)
@@ -527,7 +547,7 @@
     for inner in range(2):
         chosen = 2 * iota((FRAMES, STEPS), 0) + inner == iota((FRAMES, STEPS), 1)
         chosen = chosen.astype(bf16)
-        gb_ref[:, inner * HEADS : (inner + 1) * HEADS] = sum(mm(chosen, part) for part in raw_parts)
+        gb_ref[inner * HEADS : (inner + 1) * HEADS] = sum(mm(part, chosen, 0, 1) for part in raw_parts)
 
     for step in range(1, SEQ):
         source = (me + step) % SEQ
@@ -569,9 +589,9 @@
         out_shape=(
             jax.ShapeDtypeStruct((FRAMES, MODEL), bf16),
             jax.ShapeDtypeStruct((FRAMES, FEATURES), bf16),
-            jax.ShapeDtypeStruct((STEPS, FEATURES), bf16),
-            jax.ShapeDtypeStruct((STEPS, FEATURES), bf16),
-            jax.ShapeDtypeStruct((FRAMES, 2 * HEADS), f32),
+            jax.ShapeDtypeStruct((FRAMES, 2, FEATURES), bf16),
+            jax.ShapeDtypeStruct((FRAMES, 2, FEATURES), bf16),
+            jax.ShapeDtypeStruct((2 * HEADS, FRAMES), f32),
             jax.ShapeDtypeStruct((8, MODEL), f32),
         ),
         in_specs=[vmem] * 6,
@@ -579,6 +599,9 @@
         scratch_shapes=[
             pltpu.VMEM((STEPS, HEADS), f32),
             pltpu.VMEM((HEADS, 1, STEPS), f32),
+            pltpu.VMEM((HEADS, STEPS, DIM), bf16),
+            pltpu.VMEM((HEADS, STEPS, DIM), bf16),
+            pltpu.VMEM((2, HEADS, STEPS, STEPS), bf16),
             pltpu.VMEM((SIDE, 2, SEQ, 16, MODEL // 2), bf16),
             pltpu.VMEM((FEATURES, MODEL), bf16),
             pltpu.VMEM((SIDE, FRAMES, MODEL), bf16),
@@ -620,9 +643,9 @@
         name="delta_product",
     )(
         queries[0],
-        key_vectors[0].reshape(STEPS, FEATURES),
-        values[0].reshape(STEPS, FEATURES),
-        beta_raw[0],
+        key_vectors[0],
+        values[0],
+        beta_raw[0].T,
         cotangent[0],
         w_out,
     )
@@ -630,9 +653,9 @@
     return (
         projected[None],
         grad_query[None],
-        grad_key.reshape(1, FRAMES, 2, FEATURES),
-        grad_value.reshape(1, FRAMES, 2, FEATURES),
-        grad_raw[None],
+        grad_key[None],
+        grad_value[None],
+        grad_raw.T[None],
         grad_weight,
     )
 

time: 90.2 us -> 85.7 us (0.950)
  local copies, waits for them, and re-layouts: 11.7 us -> 5.92 us
  Pallas kernels: 77.4 us -> 78.9 us
    another operation x2 -> x0, local copies, waits for them, and re-layouts: 3.08 us -> none  [the longest x1 2.09 us: per_device(): key_vectors[0].reshape(STEPS, FEATURES)]
    reshape x2 -> x0, local copies, waits for them, and re-layouts: 3.08 us -> none  [the longest x1 2.09 us: per_device(): grad_key.reshape(1, FRAMES, 2, FEATURES)]
    pallas_call x1, Pallas kernels: 77.4 us -> 78.9 us  [per_device(): pl.pallas_call(kernel, out_shape=(jax.ShapeDtypeStruct((FRAMES, MODEL), b...]
    unnamed x15 -> x16, local copies, waits for them, and re-layouts: 5.57 us -> 5.92 us
where the time goes in v3:
time: 85.7 us; the launch traced here: 85.5 us
  Pallas kernels  78.9 us (92%)
  local copies, waits for them, and re-layouts  5.92 us (7%)
    pallas_call x1, Pallas kernels, per_device(): pl.pallas_call(kernel, out_shape=(jax.ShapeDtypeStruct((FRAMES, MODEL), b...  78.9 us
    unnamed x16, local copies, waits for them, and re-layouts  5.92 us

profile of v3, /device:TPU:0, one launch (start us, length us, event | category | flops | bytes accessed | tf_op | source)
XLA Modules:
  0.0 85.5 jit_solution(2347092168273386599)
XLA Ops:
  0.6 78.9 %delta_product.1 = (bf16[128,2048]{1,0:T(8,128)(2,1)}, bf16[128,1024]{1,0:T(8,128)(2,1)}, bf16[128,2,1024]{2,1,0:T(2,128)(2,1)}, bf16[128,2,1024]{2,1,0:T(2,128)...) custom-call(bf16[128,1024]{1,0:T(8,128)(2,1)} %bitcast.20, bf16[128,2,1024]{2,1,0:T(2,128)(2,1)} %bitcast.14, ...), custom_call_target="tpu_custom_call" | custom-call | tf_op jit(solution)/shard_map/delta_product/pallas_call | solution.py:587
  79.6 0.0 copy-start.2
  79.6 0.0 copy-start.1
  79.6 2.0 %copy.18 = bf16[1,128,2048]{2,1,0:T(8,128)(2,1)} copy(bf16[1,128,2048]{2,1,0:T(8,128)(2,1)} %bitcast.19) | data formatting | bytes 1048576
  81.6 0.0 copy-done.2
  81.6 0.7 copy.19
  82.3 0.0 copy-done.1
  82.3 0.0 copy-start
  82.3 0.8 copy.20
  83.1 0.4 copy-done
  83.5 0.0 copy-start.4
  83.5 0.0 copy-start.3
  83.5 0.8 copy.21
  84.3 0.0 copy-done.4
  84.3 0.6 copy.22
  84.9 0.0 copy-done.3
  84.9 0.6 copy.23
Async XLA Ops:
  79.6 2.0 %copy-start.2 = (bf16[128,1024]{1,0:T(8,128)(2,1)S(1)}, bf16[128,1024]{1,0:T(8,128)(2,1)}, u32[]{:S(2)}) copy-start(bf16[128,1024]{1,0:T(8,128)(2,1)} %get-tuple-element.13) | copy-start | bytes 786436
  79.6 2.7 %copy-start.1 = (bf16[128,2,1024]{2,1,0:T(2,128)(2,1)S(1)}, bf16[128,2,1024]{2,1,0:T(2,128)(2,1)}, u32[]{:S(2)}) copy-start(bf16[128,2,1024]{2,1,0:T(2,128)(2,1)} %get-tuple-element.14) | copy-start | bytes 1572868
  82.3 1.2 %copy-start = (bf16[128,2,1024]{2,1,0:T(2,128)(2,1)S(1)}, bf16[128,2,1024]{2,1,0:T(2,128)(2,1)}, u32[]{:S(2)}) copy-start(bf16[128,2,1024]{2,1,0:T(2,128)(2,1)} %get-tuple-element.15) | copy-start | bytes 1572868
  83.5 0.8 copy-start.4
  83.5 1.4 %copy-start.3 = (f32[8,2048]{1,0:T(8,128)S(1)}, f32[8,2048]{1,0:T(8,128)}, u32[]{:S(2)}) copy-start(f32[8,2048]{1,0:T(8,128)} %get-tuple-element.29) | copy-start | bytes 196612

commit v4 on v3

--- a/solution.py
+++ b/solution.py
@@ -20,8 +20,10 @@
 COLS = 512
 W_AT = 1
 RELAY_AT = 5
-WEIGHT_AT = 0
-BLOCK_AT = 1
+WEIGHT_AT = -1
+BLOCK_AT = 0
+FAR_FIRST = 1
+RELAY_SPOT = 0
 
 
 def mm(a, b, ca=1, cb=0):
@@ -231,6 +233,7 @@
     w_ring = Ring(lambda place, half: wg.at[place, c, pl.ds(8 * half, 8)], wx_ss, wx_rs)
     cot_ring = Ring(lambda place, half: cotg.at[place, pl.ds(HALF * half, HALF)], c_ss, c_rs)
     places = (x, before, after, across)
+    cot_ring.start()
 
     def core_copy(index):
         ref = wg.at[places[index], c]
@@ -320,9 +323,42 @@
 
     lax.fori_loop(0, HEADS // 2, transit_pair, 0)
     lax.fori_loop(0, HEADS // 2, reads_pair, 0)
-    w_ring.far()
-    core_copy(3).start()
-    cot_ring.start()
+    if FAR_FIRST:
+        w_ring.far()
+        core_copy(3).start()
+
+    for step in range(1, SEQ):
+        source = (me + step) % SEQ
+        arrival(t_recv.at[source], t_ss.at[source], t_rs.at[source])
+        arrival(o_recv.at[source], o_ss.at[source], o_rs.at[source])
+
+    def send_state(buffer, target, value, segment, send_sems, recv_sems):
+        buffer[segment] = value.astype(bf16)
+
+        @pl.when(segment != me)
+        def _():
+            remote(
+                buffer.at[segment], target.at[me], send_sems.at[segment], recv_sems.at[me], (dp, segment)
+            ).start()
+
+        @pl.when(segment == me)
+        def _():
+            target[me] = value.astype(bf16)
+
+    def carry_state(segment, state):
+        send_state(s_send, s_recv, state, segment, s_ss, s_rs)
+        return mm3(split(state), split(t_recv[segment]), 1, 1) + o_recv[segment].astype(f32)
+
+    empty = jnp.zeros((HALF, DIM), f32)
+    last_state = lax.fori_loop(0, SEQ - 1, carry_state, empty)
+    send_state(s_send, s_recv, last_state, SEQ - 1, s_ss, s_rs)
+
+    if not FAR_FIRST:
+        w_ring.far()
+        core_copy(3).start()
+    if RELAY_SPOT == 0:
+        cot_ring.relay()
+
 
     def order_rows(place, core):
         def one(index, carry):
@@ -374,39 +410,6 @@
 
     lax.fori_loop(0, HEADS, early_gradient, 0)
 
-    for step in range(1, SEQ):
-        source = (me + step) % SEQ
-        arrival(t_recv.at[source], t_ss.at[source], t_rs.at[source])
-        arrival(o_recv.at[source], o_ss.at[source], o_rs.at[source])
-        arrival(z_recv.at[source], z_ss.at[source], z_rs.at[source])
-
-    def send_state(buffer, target, value, segment, send_sems, recv_sems):
-        buffer[segment] = value.astype(bf16)
-
-        @pl.when(segment != me)
-        def _():
-            remote(
-                buffer.at[segment], target.at[me], send_sems.at[segment], recv_sems.at[me], (dp, segment)
-            ).start()
-
-        @pl.when(segment == me)
-        def _():
-            target[me] = value.astype(bf16)
-
-    def carry_both(index, carry):
-        state, adjoint = carry
-        last = SEQ - 1 - index
-        send_state(s_send, s_recv, state, index, s_ss, s_rs)
-        send_state(d_send, d_recv, adjoint, last, d_ss, d_rs)
-        state = mm3(split(state), split(t_recv[index]), 1, 1) + o_recv[index].astype(f32)
-        adjoint = mm3(split(adjoint), split(t_recv[last])) + z_recv[last].astype(f32)
-        return state, adjoint
-
-    empty = jnp.zeros((HALF, DIM), f32)
-    state, adjoint = lax.fori_loop(0, SEQ - 1, carry_both, (empty, empty))
-    send_state(s_send, s_recv, state, SEQ - 1, s_ss, s_rs)
-    send_state(d_send, d_recv, adjoint, 0, d_ss, d_rs)
-    cot_ring.relay()
 
     for step in range(1, SEQ):
         source = (me + step) % SEQ
@@ -433,6 +436,18 @@
         mixed_copy(step).start()
     mb_recv[0, x] = mb_send[2 * x]
     mb_recv[1, x] = mb_send[2 * x + 1]
+
+    for step in range(1, SEQ):
+        source = (me + step) % SEQ
+        arrival(z_recv.at[source], z_ss.at[source], z_rs.at[source])
+
+    def carry_adjoint(index, adjoint):
+        segment = SEQ - 1 - index
+        send_state(d_send, d_recv, adjoint, segment, d_ss, d_rs)
+        return mm3(split(adjoint), split(t_recv[segment])) + z_recv[segment].astype(f32)
+
+    first_adjoint = lax.fori_loop(0, SEQ - 1, carry_adjoint, empty)
+    send_state(d_send, d_recv, first_adjoint, 0, d_ss, d_rs)
 
     def project(index, carry):
         lanes = pl.ds(pl.multiple_of(index * COLS, COLS), COLS)

time: 85.7 us -> 77 us (0.90)
  Pallas kernels: 78.9 us -> 70.2 us
    pallas_call x1, Pallas kernels: 78.9 us -> 70.2 us  [per_device(): pl.pallas_call(kernel, out_shape=(jax.ShapeDtypeStruct((FRAMES, MODEL), b...]
where the time goes in v4:
time: 77 us; the launch traced here: 76.8 us
  Pallas kernels  70.2 us (91%)
  local copies, waits for them, and re-layouts  5.92 us (8%)
    pallas_call x1, Pallas kernels, per_device(): pl.pallas_call(kernel, out_shape=(jax.ShapeDtypeStruct((FRAMES, MODEL), b...  70.2 us
    unnamed x16, local copies, waits for them, and re-layouts  5.92 us

profile of v4, /device:TPU:0, one launch (start us, length us, event | category | flops | bytes accessed | tf_op | source)
XLA Modules:
  0.0 76.8 jit_solution(12320689701307359661)
XLA Ops:
  0.6 70.2 %delta_product.1 = (bf16[128,2048]{1,0:T(8,128)(2,1)}, bf16[128,1024]{1,0:T(8,128)(2,1)}, bf16[128,2,1024]{2,1,0:T(2,128)(2,1)}, bf16[128,2,1024]{2,1,0:T(2,128)...) custom-call(bf16[128,1024]{1,0:T(8,128)(2,1)} %bitcast.20, bf16[128,2,1024]{2,1,0:T(2,128)(2,1)} %bitcast.14, ...), custom_call_target="tpu_custom_call" | custom-call | tf_op jit(solution)/shard_map/delta_product/pallas_call | solution.py:602
  70.9 0.0 copy-start.2
  70.9 0.0 copy-start.1
  70.9 2.0 %copy.18 = bf16[1,128,2048]{2,1,0:T(8,128)(2,1)} copy(bf16[1,128,2048]{2,1,0:T(8,128)(2,1)} %bitcast.19) | data formatting | bytes 1048576
  72.8 0.0 copy-done.2
  72.8 0.7 copy.19
  73.5 0.0 copy-done.1
  73.5 0.0 copy-start
  73.5 0.8 %copy.20 = bf16[1,128,2,1024]{3,2,1,0:T(2,128)(2,1)} copy(bf16[1,128,2,1024]{3,2,1,0:T(2,128)(2,1)S(1)} %bitcast.18) | data formatting | bytes 1048576
  74.3 0.4 copy-done
  74.8 0.0 copy-start.4
  74.8 0.0 copy-start.3
  74.8 0.8 %copy.21 = bf16[1,128,2,1024]{3,2,1,0:T(2,128)(2,1)} copy(bf16[1,128,2,1024]{3,2,1,0:T(2,128)(2,1)S(1)} %bitcast.17) | data formatting | bytes 1048576
  75.6 0.0 copy-done.4
  75.6 0.6 copy.22
  76.2 0.0 copy-done.3
  76.2 0.6 copy.23
Async XLA Ops:
  70.9 2.0 %copy-start.2 = (bf16[128,1024]{1,0:T(8,128)(2,1)S(1)}, bf16[128,1024]{1,0:T(8,128)(2,1)}, u32[]{:S(2)}) copy-start(bf16[128,1024]{1,0:T(8,128)(2,1)} %get-tuple-element.13) | copy-start | bytes 786436
  70.9 2.7 %copy-start.1 = (bf16[128,2,1024]{2,1,0:T(2,128)(2,1)S(1)}, bf16[128,2,1024]{2,1,0:T(2,128)(2,1)}, u32[]{:S(2)}) copy-start(bf16[128,2,1024]{2,1,0:T(2,128)(2,1)} %get-tuple-element.14) | copy-start | bytes 1572868
  73.5 1.2 %copy-start = (bf16[128,2,1024]{2,1,0:T(2,128)(2,1)S(1)}, bf16[128,2,1024]{2,1,0:T(2,128)(2,1)}, u32[]{:S(2)}) copy-start(bf16[128,2,1024]{2,1,0:T(2,128)(2,1)} %get-tuple-element.15) | copy-start | bytes 1572868
  74.8 0.8 %copy-start.4 = (f32[16,128]{1,0:T(8,128)S(1)}, f32[16,128]{1,0:T(8,128)}, u32[]{:S(2)}) copy-start(f32[16,128]{1,0:T(8,128)} %get-tuple-element.16) | copy-start | bytes 24580
  74.8 1.4 %copy-start.3 = (f32[8,2048]{1,0:T(8,128)S(1)}, f32[8,2048]{1,0:T(8,128)}, u32[]{:S(2)}) copy-start(f32[8,2048]{1,0:T(8,128)} %get-tuple-element.29) | copy-start | bytes 196612

commit v5 on v4

--- a/solution.py
+++ b/solution.py
@@ -21,9 +21,10 @@
 W_AT = 1
 RELAY_AT = 5
 WEIGHT_AT = -1
-BLOCK_AT = 0
+BLOCK_AT = -1
 FAR_FIRST = 1
 RELAY_SPOT = 0
+PROJECT_FIRST = 0
 
 
 def mm(a, b, ca=1, cb=0):
@@ -404,13 +405,6 @@
 
     lax.fori_loop(0, HEADS // 2, gradient_pair, 0)
 
-    def early_gradient(head, carry):
-        y_s[head] = mm2((sback_s[0, head], sback_s[1, head]), gm_s[head])
-        return carry
-
-    lax.fori_loop(0, HEADS, early_gradient, 0)
-
-
     for step in range(1, SEQ):
         source = (me + step) % SEQ
         arrival(s_recv.at[source], s_ss.at[source], s_rs.at[source])
@@ -437,6 +431,12 @@
     mb_recv[0, x] = mb_send[2 * x]
     mb_recv[1, x] = mb_send[2 * x + 1]
 
+    def early_gradient(head, carry):
+        y_s[head] = mm2((sback_s[0, head], sback_s[1, head]), gm_s[head])
+        return carry
+
+    lax.fori_loop(0, HEADS, early_gradient, 0)
+
     for step in range(1, SEQ):
         source = (me + step) % SEQ
         arrival(z_recv.at[source], z_ss.at[source], z_rs.at[source])
@@ -454,7 +454,8 @@
         proj_ref[:, lanes] = mm(mb_full[...], wf[:, lanes]).astype(bf16)
         return carry
 
-    lax.fori_loop(0, MODEL // COLS, project, 0)
+    if PROJECT_FIRST:
+        lax.fori_loop(0, MODEL // COLS, project, 0)
 
     def weight_chunk(inner, chunk):
         mixed = mb_recv[inner].reshape(SIDE * FRAMES, DIM)
@@ -484,13 +485,29 @@
     if WEIGHT_AT < 0:
         weight_parts()
 
-    for step in range(1, SEQ):
-        source = (me + step) % SEQ
-        arrival(d_recv.at[source], d_ss.at[source], d_rs.at[source])
 
     def block_copy(step):
         to = (me + step) % SEQ
         return remote(gws.at[to], gwb.at[me], b_ss.at[to], b_rs.at[me], (dp, to))
+
+    def send_blocks():
+        for chunk in range(MODEL // COLS):
+            lanes = pl.ds(chunk * COLS, COLS)
+            arrival(gwr.at[:, lanes], g_ss.at[chunk], g_rs.at[chunk])
+
+        def one(index, carry):
+            rows = pl.ds(pl.multiple_of(index * 16, 16), 16)
+            block = gwp[rows] + gwr[rows].astype(f32)
+            for inner in range(2):
+                part = block[8 * inner : 8 * inner + 8]
+                halves = [part[:, : MODEL // 2], part[:, MODEL // 2 :]]
+                gws[2 * index + inner] = jnp.concatenate(halves, axis=0).astype(bf16)
+            return carry
+
+        lax.fori_loop(0, SEQ // 2, one, 0)
+        for step in range(1, SEQ):
+            block_copy(step).start()
+        gwb[me] = gws[me]
 
     def backward_head(head, raw_all):
         queries, keys = q_ref[:, head_lanes(head)], k_s[head]
@@ -523,6 +540,14 @@
         gk_ref[:, :, head_lanes(head)] = key_grad.reshape(FRAMES, 2, DIM)
         return raw_grad
 
+    if not PROJECT_FIRST:
+        lax.fori_loop(0, MODEL // COLS, project, 0)
+    if BLOCK_AT < 0:
+        send_blocks()
+    for step in range(1, SEQ):
+        source = (me + step) % SEQ
+        arrival(d_recv.at[source], d_ss.at[source], d_rs.at[source])
+
     lane = iota((STEPS, HEADS), 1)
 
     def backward_pair(index, total):
@@ -537,23 +562,7 @@
 
         @pl.when(index == BLOCK_AT)
         def _():
-            for chunk in range(MODEL // COLS):
-                lanes = pl.ds(chunk * COLS, COLS)
-                arrival(gwr.at[:, lanes], g_ss.at[chunk], g_rs.at[chunk])
-
-            def one(index, carry):
-                rows = pl.ds(pl.multiple_of(index * 16, 16), 16)
-                block = gwp[rows] + gwr[rows].astype(f32)
-                for inner in range(2):
-                    part = block[8 * inner : 8 * inner + 8]
-                    halves = [part[:, : MODEL // 2], part[:, MODEL // 2 :]]
-                    gws[2 * index + inner] = jnp.concatenate(halves, axis=0).astype(bf16)
-                return carry
-
-            lax.fori_loop(0, SEQ // 2, one, 0)
-            for step in range(1, SEQ):
-                block_copy(step).start()
-            gwb[me] = gws[me]
+            send_blocks()
 
         return total
 

time: 77 us -> 76.3 us (level)
  no operation moved by 1% of the time
where the time goes in v5:
time: 76.3 us; the launch traced here: 76.1 us
  Pallas kernels  69.5 us (91%)
  local copies, waits for them, and re-layouts  5.92 us (8%)
    pallas_call x1, Pallas kernels, per_device(): pl.pallas_call(kernel, out_shape=(jax.ShapeDtypeStruct((FRAMES, MODEL), b...  69.5 us
    unnamed x16, local copies, waits for them, and re-layouts  5.92 us

profile of v5, /device:TPU:0, one launch (start us, length us, event | category | flops | bytes accessed | tf_op | source)
XLA Modules:
  0.0 76.1 jit_solution(14737492489594926209)
XLA Ops:
  0.6 69.5 %delta_product.1 = (bf16[128,2048]{1,0:T(8,128)(2,1)}, bf16[128,1024]{1,0:T(8,128)(2,1)}, bf16[128,2,1024]{2,1,0:T(2,128)(2,1)}, bf16[128,2,1024]{2,1,0:T(2,128)...) custom-call(bf16[128,1024]{1,0:T(8,128)(2,1)} %bitcast.20, bf16[128,2,1024]{2,1,0:T(2,128)(2,1)} %bitcast.14, ...), custom_call_target="tpu_custom_call" | custom-call | tf_op jit(solution)/shard_map/delta_product/pallas_call | solution.py:611
  70.1 0.0 copy-start.2
  70.2 0.0 copy-start.1
  70.2 2.0 %copy.18 = bf16[1,128,2048]{2,1,0:T(8,128)(2,1)} copy(bf16[1,128,2048]{2,1,0:T(8,128)(2,1)} %bitcast.19) | data formatting | bytes 1048576
  72.1 0.0 copy-done.2
  72.1 0.7 copy.19
  72.8 0.0 copy-done.1
  72.8 0.0 copy-start
  72.8 0.8 %copy.20 = bf16[1,128,2,1024]{3,2,1,0:T(2,128)(2,1)} copy(bf16[1,128,2,1024]{3,2,1,0:T(2,128)(2,1)S(1)} %bitcast.18) | data formatting | bytes 1048576
  73.6 0.4 copy-done
  74.1 0.0 copy-start.4
  74.1 0.0 copy-start.3
  74.1 0.8 %copy.21 = bf16[1,128,2,1024]{3,2,1,0:T(2,128)(2,1)} copy(bf16[1,128,2,1024]{3,2,1,0:T(2,128)(2,1)S(1)} %bitcast.17) | data formatting | bytes 1048576
  74.9 0.0 copy-done.4
  74.9 0.6 copy.22
  75.5 0.0 copy-done.3
  75.5 0.6 copy.23
Async XLA Ops:
  70.1 2.0 %copy-start.2 = (bf16[128,1024]{1,0:T(8,128)(2,1)S(1)}, bf16[128,1024]{1,0:T(8,128)(2,1)}, u32[]{:S(2)}) copy-start(bf16[128,1024]{1,0:T(8,128)(2,1)} %get-tuple-element.13) | copy-start | bytes 786436
  70.2 2.7 %copy-start.1 = (bf16[128,2,1024]{2,1,0:T(2,128)(2,1)S(1)}, bf16[128,2,1024]{2,1,0:T(2,128)(2,1)}, u32[]{:S(2)}) copy-start(bf16[128,2,1024]{2,1,0:T(2,128)(2,1)} %get-tuple-element.14) | copy-start | bytes 1572868
  72.8 1.2 %copy-start = (bf16[128,2,1024]{2,1,0:T(2,128)(2,1)S(1)}, bf16[128,2,1024]{2,1,0:T(2,128)(2,1)}, u32[]{:S(2)}) copy-start(bf16[128,2,1024]{2,1,0:T(2,128)(2,1)} %get-tuple-element.15) | copy-start | bytes 1572868
  74.1 0.8 %copy-start.4 = (f32[16,128]{1,0:T(8,128)S(1)}, f32[16,128]{1,0:T(8,128)}, u32[]{:S(2)}) copy-start(f32[16,128]{1,0:T(8,128)} %get-tuple-element.16) | copy-start | bytes 24580
  74.1 1.4 %copy-start.3 = (f32[8,2048]{1,0:T(8,128)S(1)}, f32[8,2048]{1,0:T(8,128)}, u32[]{:S(2)}) copy-start(f32[8,2048]{1,0:T(8,128)} %get-tuple-element.29) | copy-start | bytes 196612
